TPU v7x, 128 devices: a whole 4x4x4 slice. The times are simulated.
128 devices in a mesh: group: 16 (over x, z_hi, core), head: 8 (over y, z_lo).
Axes of the slice: x: 4, y: 4, z: 4 (z_hi: 2, z_lo: 2; z = z_hi * 2 + z_lo), core: 2. Of those that a mesh axis runs over, the one named last changes fastest.
Arguments:
- queries: bfloat16 [4096, 5120], P('group', 'head'), may hold values from -8 to 8
- keys: bfloat16 [4096, 5120], P('group', 'head'), may hold values from -6 to 6
- values: bfloat16 [4096, 5120], P('group', 'head'), may hold values from -6 to 6
- text_keys: bfloat16 [512, 5120], P(None, 'head'), may hold values from -8 to 8
- text_values: bfloat16 [512, 5120], P(None, 'head'), may hold values from -6 to 6
- d_out: bfloat16 [4096, 5120], P('group', 'head'), may hold values from -6 to 6
- gain_q: bfloat16 [5120], P('head'), may hold values from 0.099609375 to 1.8984375
- gain_k: bfloat16 [5120], P('head'), may hold values from 0.099609375 to 1.8984375
- group_of: int32 [16], replicated, may hold values from 0 to 15, each once
Outputs:
- d_queries: bfloat16 [4096, 5120], P('group', 'head')
- d_keys: bfloat16 [4096, 5120], P('group', 'head')
- d_values: bfloat16 [4096, 5120], P('group', 'head')
- d_text_keys: bfloat16 [512, 5120], P(None, 'head')
- d_text_values: bfloat16 [512, 5120], P(None, 'head')
Inputs may be any that keep to these rules, and one draw needn't show every extreme that they name: `group_of`: each group number appears once.
All inputs are finite; a program needn't handle non-finite values.
Results may differ from a plain program's by a relative error of at most 0.014.
The roundings to bfloat16 on the way count: a program that leaves them out, or rounds other values in their place, can miss the bound.
Values may be sent and summed in bfloat16 or wider, within the bound.
A program may use at most 128 MiB of HBM per device.

v0:
```python
import jax
import jax.numpy as jnp
from jax import lax
from jax.sharding import PartitionSpec as P

DH = 128


EPS = 1e-06


def split_heads(x, size):
    return x.reshape(x.shape[0], x.shape[1] // size, size)


def tile_scores(q_three, k_three, shown, scale):
    scores = (
        jnp.einsum("qhd,khd->hqk", q_three, k_three, preferred_element_type=jnp.float32) * scale
    )
    return jnp.where(shown, scores, -jnp.inf)


def tile_grads(q_three, k_three, v_three, g_three, shown, lse, delta, scale):
    scores = tile_scores(q_three, k_three, shown, scale)
    probs = jnp.exp(scores - lse[:, :, None])
    soft = probs.astype(jnp.bfloat16)
    d_probs = jnp.einsum("qhd,khd->hqk", g_three, v_three, preferred_element_type=jnp.float32)
    d_scores = (probs * (d_probs - delta[:, :, None]) * scale).astype(jnp.bfloat16)
    return (soft, d_scores)


def body(queries, keys, values, text_keys, text_values, d_out, gain_q, gain_k, group_of):
    rows, width = queries.shape
    scale = DH ** (-0.5)
    full = width * lax.axis_size("head")
    my_group = group_of[lax.axis_index("group")]
    q_float = queries.astype(jnp.float32)
    k_float = keys.astype(jnp.float32)
    gains_q = gain_q.astype(jnp.float32)
    gains_k = gain_k.astype(jnp.float32)
    squares = lax.psum(
        (jnp.sum(q_float * q_float, axis=-1), jnp.sum(k_float * k_float, axis=-1)), "head"
    )
    scale_q = lax.rsqrt(squares[0] / full + EPS)
    scale_k = lax.rsqrt(squares[1] / full + EPS)
    q_norm = (q_float * scale_q[:, None] * gains_q).astype(jnp.bfloat16)
    k_norm = (k_float * scale_k[:, None] * gains_k).astype(jnp.bfloat16)
    k_every, v_every = (
        lax.all_gather(k_norm, "group", axis=0, tiled=True),
        lax.all_gather(values, "group", axis=0, tiled=True),
    )
    total = k_every.shape[0]
    block = min(512, total)
    nblocks = total // block
    key_groups = group_of[jnp.arange(total, dtype=jnp.int32) // rows]
    q_three = split_heads(q_norm, DH)
    g_three = split_heads(d_out, DH)
    text_k3 = split_heads(text_keys, DH)
    text_v3 = split_heads(text_values, DH)
    indices = jnp.arange(nblocks, dtype=jnp.int32)

    def block_of(index):
        start = index * block
        k_block = split_heads(lax.dynamic_slice_in_dim(k_every, start, block, 0), DH)
        v_block = split_heads(lax.dynamic_slice_in_dim(v_every, start, block, 0), DH)
        shown = lax.dynamic_slice_in_dim(key_groups, start, block, 0) <= my_group
        return (k_block, v_block, shown)

    text_scores = (
        jnp.einsum("qhd,khd->hqk", q_three, text_k3, preferred_element_type=jnp.float32) * scale
    )
    top_text = jnp.max(text_scores, axis=-1)
    sum_text = jnp.sum(jnp.exp(text_scores - top_text[:, :, None]), axis=-1)

    def max_step(carry, index):
        k_block, v_block, shown = block_of(index)
        scores = tile_scores(q_three, k_block, shown[None, None, :], scale)
        top = jnp.maximum(carry[0], jnp.max(scores, axis=-1))
        summed = carry[1] * jnp.exp(carry[0] - top) + jnp.sum(
            jnp.exp(scores - top[:, :, None]), axis=-1
        )
        return ((top, summed), None)

    (top_all, sum_all), _ = lax.scan(max_step, (top_text, sum_text), indices)
    lse = top_all + jnp.log(sum_all)
    text_probs = jnp.exp(text_scores - lse[:, :, None])
    text_soft = text_probs.astype(jnp.bfloat16)
    out_text = jnp.einsum("hqk,khd->qhd", text_soft, text_v3, preferred_element_type=jnp.float32)

    def out_step(acc, index):
        k_block, v_block, shown = block_of(index)
        scores = tile_scores(q_three, k_block, shown[None, None, :], scale)
        soft = jnp.exp(scores - lse[:, :, None]).astype(jnp.bfloat16)
        return (
            acc + jnp.einsum("hqk,khd->qhd", soft, v_block, preferred_element_type=jnp.float32),
            None,
        )

    out_sum, _ = lax.scan(out_step, out_text, indices)
    out_round = lax.optimization_barrier(out_sum.astype(jnp.bfloat16))
    delta = jnp.sum(g_three.astype(jnp.float32) * out_round.astype(jnp.float32), axis=-1).T
    text_dp = jnp.einsum("qhd,khd->hqk", g_three, text_v3, preferred_element_type=jnp.float32)
    text_ds = (text_probs * (text_dp - delta[:, :, None]) * scale).astype(jnp.bfloat16)
    dq_text = jnp.einsum("hqk,khd->qhd", text_ds, text_k3, preferred_element_type=jnp.float32)
    part_tk = jnp.einsum(
        "hqk,qhd->khd", text_ds, q_three, preferred_element_type=jnp.float32
    ).reshape(-1, width)
    part_tv = jnp.einsum(
        "hqk,qhd->khd", text_soft, g_three, preferred_element_type=jnp.float32
    ).reshape(-1, width)
    text_sums = lax.psum((part_tk, part_tv), "group")

    def back_step(acc, index):
        k_block, v_block, shown = block_of(index)
        soft, d_scores = tile_grads(
            q_three, k_block, v_block, g_three, shown[None, None, :], lse, delta, scale
        )
        new_acc = acc + jnp.einsum(
            "hqk,khd->qhd", d_scores, k_block, preferred_element_type=jnp.float32
        )
        grad_key = jnp.einsum("hqk,qhd->khd", d_scores, q_three, preferred_element_type=jnp.float32)
        grad_value = jnp.einsum("hqk,qhd->khd", soft, g_three, preferred_element_type=jnp.float32)
        new_acc, grad_key, grad_value = (new_acc, grad_key, grad_value)
        joined = jnp.concatenate(
            [grad_key.reshape(block, width), grad_value.reshape(block, width)], axis=1
        )
        return (new_acc, joined)

    dq_three, terms = lax.scan(back_step, dq_text, indices)
    terms = terms.reshape(total, 2 * width)
    key_terms = lax.psum_scatter(terms, "group", scatter_dimension=0, tiled=True)
    dk_norm = key_terms[:, :width]
    dv_sum = key_terms[:, width:]
    grad_q = dq_three.reshape(rows, width) * gains_q
    grad_k = dk_norm * gains_k
    inner = lax.psum(
        (jnp.sum(q_float * grad_q, axis=-1), jnp.sum(k_float * grad_k, axis=-1)), "head"
    )
    d_queries = scale_q[:, None] * grad_q - q_float * (scale_q**3 * inner[0] / full)[:, None]
    d_keys = scale_k[:, None] * grad_k - k_float * (scale_k**3 * inner[1] / full)[:, None]
    return (
        d_queries.astype(jnp.bfloat16),
        d_keys.astype(jnp.bfloat16),
        dv_sum.astype(jnp.bfloat16),
        text_sums[0].astype(jnp.bfloat16),
        text_sums[1].astype(jnp.bfloat16),
    )


def solution(mesh):
    placed = (
        P("group", "head"),
        P("group", "head"),
        P("group", "head"),
        P(None, "head"),
        P(None, "head"),
        P("group", "head"),
        P("head"),
        P("head"),
        P(),
    )
    return jax.shard_map(
        body,
        mesh=mesh,
        in_specs=placed,
        out_specs=(
            P("group", "head"),
            P("group", "head"),
            P("group", "head"),
            P(None, "head"),
            P(None, "head"),
        ),
        check_vma=False,
    )
```

profile of v0, /device:TPU:4, one launch (start us, length us, event | category | flops | bytes accessed | tf_op | source)
XLA Modules:
  0.0 550.0 jit_solution(9563791224431190386)
XLA Ops:
  10.4 20.4 %all-reduce.2 = (f32[256]{0:T(256)S(1)}, f32[256]{0:T(256)S(1)}) all-reduce(f32[256]{0:T(256)S(1)} %fusion.24, f32[256]{0:T(256)S(1)} %fusion.30), channel_id=1, replica_groups=mesh['group'=16,'head'=8] {'head'}, use_global_device_ids=true, to_apply=%region_1.0 | all-reduce | flops 512 | bytes 4096 | tf_op jit(solution)/shard_map/psum | solution.py:41
  35.9 4.3 compare_select_fusion.1
  44.9 5.7 %select_select_fusion = s32[4096]{0:T(1024)S(1)} fusion(pred[4096]{0:T(1024)(128)(4,1)S(1)} %compare_reduce_fusion, pred[4096]{0:T(1024)(128)(4,1)S(1)} %compare_reduce_fusion.1, pred[4096]{0:T(1024)(128)(4,1)S(1)} %compare_reduce_fusion.2, pred[4096]{0:T(1024)(128)(4,1)S(1)} %compare_reduce_fusion.3, pred[4096]{0:T(1024)(128)(4,1)S(1)} %compare_reduce_fusion.4, ...), kind=kLoop, calls=%fused_computation.91 | loop fusion | flops 36864 | bytes 69668 | tf_op jit(solution)/shard_map/gather | solution.py:55
  53.1 37.5 %all-gather.3.cloned.1.call-done = bf16[4096,640]{1,0:T(8,128)(2,1)} async-done(((bf16[256,640]{1,0:T(8,128)(2,1)}), bf16[4096,640]{1,0:T(8,128)(2,1)}) %all-gather.3.cloned.1.call-update) | async-done | bytes 5242896 | tf_op jit(solution)/shard_map/all_gather | solution.py:49
  90.6 7.9 %copy.43 = bf16[4096,640]{0,1:T(8,128)(2,1)} copy(bf16[4096,640]{1,0:T(8,128)(2,1)} %all-gather.3.cloned.1.call-done) | data formatting | bytes 10485760 | tf_op jit(solution)/shard_map/while | solution.py:84
  98.5 43.1 %while.34 = (s32[]{:T(128)}, f32[5,256]{1,0:T(8,128)S(1)}, f32[5,256]{1,0:T(8,128)S(1)}, s32[8]{0:T(128)S(1)}, s32[4096]{0:T(1024)S(1)}, /*index=5*/s32[]{:T(128...) while((s32[]{:T(128)}, f32[5,256]{1,0:T(8,128)S(1)}, ...), condition=%wide.region_9.10_spmd, body=%wide.region_6.9_spmd.sunk | while | flops 172362752 | bytes 7606979 | solution.py:84
  141.6 2.6 convolution_bitcast_fusion.2
  144.2 2.2 copy.51
  146.4 9.1 %all-gather.5.cloned.1.call-done = bf16[4096,640]{0,1:T(8,128)(2,1)} async-done(((bf16[256,640]{0,1:T(8,128)(2,1)}), bf16[4096,640]{0,1:T(8,128)(2,1)}) %all-gather.5.cloned.1.call-update) | async-done | bytes 5242896 | tf_op jit(solution)/shard_map/all_gather | solution.py:50
  155.6 63.3 %while.35 = (s32[]{:T(128)}, f32[256,5,128]{0,2,1:T(8,128)}, s32[8]{0:T(128)S(1)}, bf16[4096,640]{0,1:T(8,128)(2,1)}, s32[4096]{0:T(1024)S(1)}, /*index=5*/s32[]...) while((s32[]{:T(128)}, f32[256,5,128]{0,2,1:T(8,128)}, ...), condition=%wide.region_11.12_spmd, body=%wide.region_10.11_spmd.sunk | while | flops 338330112 | bytes 5578955 | solution.py:99
  157.5 2.4 constant_dynamic-slice_fusion.9
  159.9 3.5 fusion.99
  165.4 2.4 constant_dynamic-slice_fusion.9
  167.9 3.5 fusion.99
  173.3 2.4 constant_dynamic-slice_fusion.9
  175.8 3.5 fusion.99
  181.2 2.4 constant_dynamic-slice_fusion.9
  183.7 3.5 fusion.99
  189.2 2.4 constant_dynamic-slice_fusion.9
  191.6 3.5 fusion.99
  197.1 2.4 constant_dynamic-slice_fusion.9
  199.5 3.5 fusion.99
  205.0 2.4 constant_dynamic-slice_fusion.9
  207.4 3.5 fusion.99
  212.9 2.4 constant_dynamic-slice_fusion.9
  215.3 3.5 fusion.99
  224.0 103.2 %while.36 = (s32[]{:T(128)}, f32[256,5,128]{0,2,1:T(8,128)S(1)}, f32[8,512,1280]{2,1,0:T(8,128)}, s32[8]{0:T(128)S(1)}, bf16[4096,640]{0,1:T(8,128)(2,1)}, /*ind...) while((s32[]{:T(128)}, f32[256,5,128]{0,2,1:T(8,128)S(1)}, ...), condition=%wide.region_14.15_spmd, body=%wide.region_13.14_spmd.sunk | while | flops 846889472 | bytes 42617628 | solution.py:129
  231.3 2.1 copy.87
  233.4 3.5 constant_dynamic-update-slice_fusion.2
  244.2 2.1 copy.87
  246.3 3.5 constant_dynamic-update-slice_fusion.2
  257.2 2.1 copy.87
  259.3 3.5 constant_dynamic-update-slice_fusion.2
  270.1 2.1 copy.87
  272.2 3.5 constant_dynamic-update-slice_fusion.2
  283.0 2.1 copy.87
  285.1 3.5 constant_dynamic-update-slice_fusion.2
  295.9 2.1 copy.87
  298.0 3.4 constant_dynamic-update-slice_fusion.2
  308.8 2.1 copy.87
  310.9 3.4 constant_dynamic-update-slice_fusion.2
  321.7 2.1 copy.87
  323.8 3.4 constant_dynamic-update-slice_fusion.2
  331.6 2.9 copy.59
  335.9 3.3 copy.58
  339.4 92.4 %all-reduce.4 = (bf16[512,640]{1,0:T(8,128)(2,1)}, bf16[512,640]{1,0:T(8,128)(2,1)}) all-reduce(f32[512,640]{1,0:T(8,128)} %copy.58, f32[512,640]{1,0:T(8,128)S(1)} %copy-done.12), channel_id=1, replica_groups=mesh['group'=16,'head'=8] {'group'}, use_global_device_ids=true, to_apply=%region_20.21 | all-reduce | flops 655360 | bytes 3932160 | tf_op jit(solution)/shard_map/psum | solution.py:111
  431.9 88.7 %reduce-scatter.2.cloned.1.call-done = f32[256,1280]{1,0:T(8,128)} async-done(((f32[4096,1280]{1,0:T(8,128)}), f32[256,1280]{1,0:T(8,128)}) %reduce-scatter.2.cloned.1.call-update) | async-done | bytes 1310736 | tf_op jit(solution)/shard_map/reduce_scatter | solution.py:131
  521.9 18.8 %all-reduce.1 = (f32[256]{0:T(256)S(1)}, f32[256]{0:T(256)S(1)}) all-reduce(f32[256]{0:T(256)S(1)} %fusion.27, f32[256]{0:T(256)S(1)} %fusion.33), channel_id=1, replica_groups=mesh['group'=16,'head'=8] {'head'}, use_global_device_ids=true, to_apply=%region_16.17 | all-reduce | flops 512 | bytes 4096 | tf_op jit(solution)/shard_map/psum | solution.py:136
  (271 shorter events, 131.2 us)
Async XLA Ops:
  7.2 27.8 %copy-start.18 = (bf16[640]{0:T(1024)(128)(2,1)S(1)}, bf16[640]{0:T(1024)(128)(2,1)}, u32[]{:S(2)}) copy-start(bf16[640]{0:T(1024)(128)(2,1)} %param.21) | copy-start | bytes 3844
  7.2 27.9 %copy-start.17 = (s32[16]{0:T(128)S(1)}, s32[16]{0:T(128)}, u32[]{:S(2)}) copy-start(s32[16]{0:T(128)} %param.23) | copy-start | bytes 196
  7.2 83.4 %all-gather.3.cloned.1.call-start = ((), (), s32[]{:S(2)}) async-start(), calls=%async_computation.1 | async-start | bytes 5570560 | tf_op jit(solution)/shard_map/all_gather | solution.py:49
  9.0 33.2 %copy-start.16 = (bf16[256,640]{1,0:T(8,128)(2,1)S(1)}, bf16[256,640]{1,0:T(8,128)(2,1)}, u32[]{:S(2)}) copy-start(bf16[256,640]{1,0:T(8,128)(2,1)} %param.20) | copy-start | bytes 983044
  10.2 32.0 %copy-start.8 = (bf16[256,640]{0,1:T(8,128)(2,1)}, bf16[256,640]{0,1:T(8,128)(2,1)S(1)}, u32[]{:S(2)}) copy-start(bf16[256,640]{0,1:T(8,128)(2,1)S(1)} %copy.39) | copy-start | bytes 983044
  10.2 32.2 %copy-start.14 = (bf16[512,640]{1,0:T(8,128)(2,1)S(1)}, bf16[512,640]{1,0:T(8,128)(2,1)}, u32[]{:S(2)}) copy-start(bf16[512,640]{1,0:T(8,128)(2,1)} %param.18) | copy-start | bytes 1966084
  32.7 10.9 %copy-start.15 = (bf16[512,640]{1,0:T(8,128)(2,1)S(1)}, bf16[512,640]{1,0:T(8,128)(2,1)}, u32[]{:S(2)}) copy-start(bf16[512,640]{1,0:T(8,128)(2,1)} %param.19) | copy-start | bytes 1966084
  32.7 122.8 %all-gather.5.cloned.1.call-start = ((), (), s32[]{:S(2)}) async-start(), calls=%async_computation.2 | async-start | bytes 5570560 | tf_op jit(solution)/shard_map/all_gather | solution.py:50
  34.7 485.9 %reduce-scatter.2.cloned.1.call-start = ((), (), s32[]{:S(2)}) async-start(), calls=%async_computation.3 | async-start | bytes 22282240 | tf_op jit(solution)/shard_map/reduce_scatter | solution.py:131
  52.3 167.8 %copy-start = (f32[5,256,512]{2,1,0:T(8,128)}, f32[5,256,512]{2,1,0:T(8,128)S(1)}, u32[]{:S(2)}) copy-start(f32[5,256,512]{2,1,0:T(8,128)S(1)} %get-tuple-element.314) | copy-start | bytes 7864324
  220.1 3.2 copy-start.10
  222.2 1.1 copy-start.6
  230.3 0.8 copy-start.2
  233.4 3.5 copy-start.3
  243.2 0.8 copy-start.2
  246.3 3.5 copy-start.3
  256.1 0.8 copy-start.2
  259.3 3.5 copy-start.3
  269.0 0.8 copy-start.2
  272.2 3.5 copy-start.3
  282.0 0.8 copy-start.2
  285.1 3.5 copy-start.3
  294.9 0.8 copy-start.2
  298.0 3.4 copy-start.3
  307.7 0.8 copy-start.2
  310.9 3.5 copy-start.3
  320.6 0.8 copy-start.2
  323.8 3.4 copy-start.3
  327.2 0.8 copy-start.4
  328.0 1.7 copy-start.1
  331.6 2.9 copy-start.7
  334.5 4.8 copy-start.5
  334.5 4.8 copy-start.9
  335.9 3.5 copy-start.12
  335.9 184.7 %copy-start.11 = (bf16[256,640]{1,0:T(8,128)(2,1)S(1)}, bf16[256,640]{1,0:T(8,128)(2,1)}, u32[]{:S(2)}) copy-start(bf16[256,640]{1,0:T(8,128)(2,1)} %param.16) | copy-start | bytes 983044
  520.6 21.2 %copy-start.13 = (f32[256,1280]{1,0:T(8,128)S(1)}, f32[256,1280]{1,0:T(8,128)}, u32[]{:S(2)}) copy-start(f32[256,1280]{1,0:T(8,128)} %reduce-scatter.2.cloned.1.call-done) | copy-start | bytes 3932164
Sparse Core Ops, SparseCore 0:
  32.8 57.7 all-gather.2
  92.8 62.6 all-gather.4
  328.2 192.3 reduce-scatter.1
where the time goes:
time: 554 us; the launch traced here: 550 us
  waiting for transfers between devices  135 us (24%)
  blocking collectives  132 us (24%)
  local copies, waits for them, and re-layouts  130 us (23%)
  matrix products  78.9 us (14%)
  other arithmetic  42.9 us (8%)
  loops' own time  16.6 us (3%)
  between operations  14 us (3%)
    psum x1, blocking collectives, body(): text_sums = lax.psum((part_tk, part_tv), 'group')  92.4 us
    reduce_scatter x1, waiting for transfers between devices, body(): lax.psum_scatter(terms, 'group', scatter_dimension=0, tiled=True)  88.7 us
    dynamic_update_slice x16, local copies, waits for them, and re-layouts, body(): dq_three, terms = lax.scan(back_step, dq_text, indices)  44.5 us
    all_gather x1, waiting for transfers between devices, body(): lax.all_gather(k_norm, 'group', axis=0, tiled=True)  37.5 us
    dynamic_slice x16, local copies, waits for them, and re-layouts, block_of(): lax.dynamic_slice_in_dim(k_every, start, block, 0)  28.6 us
    dot_general x8, matrix products, out_step(): jnp.einsum('hqk,khd->qhd', soft, v_block, preferred_element_type=jnp.floa...  28.1 us
    psum x1, blocking collectives, body(): lax.psum((jnp.sum(q_float * q_float, axis=-1), jnp.sum(k_float * k_float,...  20.4 us
    psum x1, blocking collectives, body(): lax.psum((jnp.sum(q_float * grad_q, axis=-1), jnp.sum(k_float * grad_k, a...  18.8 us
  transfers between devices with their start and end apart: 3, of which 3 were waited for; matrix products, arithmetic and copies ran while one was open for 15% of the time, Pallas kernels for 0%

commit v1 on v0

v1 whole, which is shorter than its diff:
```python
import functools
import math

import jax
import jax.numpy as jnp
from jax import lax
from jax.experimental import pallas as pl
from jax.experimental.pallas import tpu as pltpu
from jax.sharding import PartitionSpec as P

DH = 128
EPS = 1e-06
BLK = 256
NG = 16
NH = 5
NDEV = 15
WIN = 96
ROWS = 1408
QPAD = 1552
TWIN = 176
SCALE = DH ** (-0.5)
MESH = pl.DeviceIdType.MESH
F32 = jnp.float32
BF16 = jnp.bfloat16
VMEM_LIMIT = 56 * 1024 * 1024


def greet(me, hd, nh):
    barrier = pltpu.get_barrier_semaphore()
    for d in range(1, NG):
        pl.semaphore_signal(
            barrier, inc=1, device_id={"group": lax.rem(me + d, NG)}, device_id_type=MESH
        )
    for d in range(1, nh):
        pl.semaphore_signal(
            barrier, inc=1, device_id={"head": lax.rem(hd + d, nh)}, device_id_type=MESH
        )
    pl.semaphore_wait(barrier, NG - 1 + nh - 1)


def row_sums(acc):
    return jnp.sum(acc.T, axis=0, keepdims=True)


def as_column(row):
    return jnp.broadcast_to(row, (DH, BLK)).T


def head_sum(row_q, row_k, send, recv, send_sem, recv_sem, hd, nh):
    send[...] = jnp.concatenate([row_q, row_k, jnp.zeros((6, BLK), F32)], axis=0)
    copies = []
    for d in range(1, nh):
        peer = lax.rem(hd + d, nh)
        copy = pltpu.make_async_remote_copy(
            src_ref=send,
            dst_ref=recv.at[d],
            send_sem=send_sem.at[d],
            recv_sem=recv_sem.at[d],
            device_id={"head": peer},
            device_id_type=MESH,
        )
        copy.start()
        copies.append(copy)
    return copies


def head_total(copies, send, recv, nh):
    for copy in copies:
        copy.wait()
    total = send[...]
    for d in range(1, nh):
        total = total + recv[d]
    return total


def spread_kernel(
    nh, q_ref, k_ref, v_ref, g_ref, gain_q, gain_k,
    kall, vall, qall, gall, scales,
    qn, kn, sq_send, sq_recv, send_sem, recv_sem, local_sem, ss, rs,
):
    me = lax.axis_index("group")
    hd = lax.axis_index("head")
    greet(me, hd, nh)

    def whole(ref, out, kind, t):
        head = lax.div(t, 3)
        cols = pl.ds(pl.multiple_of(head * DH, DH), DH)
        return ref.at[:, cols], out.at[pl.ds(pl.multiple_of(me * BLK, BLK), BLK)]

    def third(ref, out, kind, t):
        head = lax.div(t, 3)
        part = lax.rem(t, 3)
        cols = pl.ds(pl.multiple_of(head * DH, DH), DH)
        src = ref.at[pl.ds(pl.multiple_of(part * 80, 16), WIN), cols]
        return src, out.at[pl.ds(pl.multiple_of(me * WIN, WIN), WIN)]

    plan = ((whole, v_ref, vall), (third, g_ref, gall), (whole, kn, kall), (third, qn, qall))

    def remote(kind, t):
        form, ref, out = plan[kind]
        src, dst = form(ref, out, kind, t)
        return pltpu.make_async_remote_copy(
            src_ref=src,
            dst_ref=dst,
            send_sem=send_sem.at[kind, t],
            recv_sem=recv_sem.at[kind, me],
            device_id={"group": t},
            device_id_type=MESH,
        )

    def local(kind):
        form, ref, out = plan[kind]
        src, dst = form(ref, out, kind, me)
        return pltpu.make_async_copy(src, dst, local_sem.at[kind])

    def send_all(kinds):
        @pl.loop(1, NG)
        def _(d):
            t = lax.rem(me + d, NG)

            @pl.when(t < NDEV)
            def _():
                for kind in kinds:
                    remote(kind, t).start()

        @pl.when(me < NDEV)
        def _():
            for kind in kinds:
                local(kind).start()

    acc_q = jnp.zeros((BLK, DH), F32)
    acc_k = jnp.zeros((BLK, DH), F32)
    for h in range(NH):
        cols = slice(h * DH, (h + 1) * DH)
        x = q_ref[:, cols].astype(F32)
        acc_q = acc_q + x * x
        x = k_ref[:, cols].astype(F32)
        acc_k = acc_k + x * x
    copies = head_sum(row_sums(acc_q), row_sums(acc_k), sq_send, sq_recv, ss, rs, hd, nh)
    send_all((0, 1))
    total = head_total(copies, sq_send, sq_recv, nh)
    scale = lax.rsqrt(total / (NH * DH * nh) + EPS)
    scales[...] = scale
    col_q = as_column(scale[0:1])
    col_k = as_column(scale[1:2])
    for h in range(NH):
        cols = slice(h * DH, (h + 1) * DH)
        kn[:, cols] = (k_ref[:, cols].astype(F32) * col_k * gain_k[:, cols].astype(F32)).astype(BF16)
        qn[:, cols] = (q_ref[:, cols].astype(F32) * col_q * gain_q[:, cols].astype(F32)).astype(BF16)
    send_all((2, 3))

    @pl.loop(1, NG)
    def _(d):
        t = lax.rem(me + d, NG)

        @pl.when(t < NDEV)
        def _():
            for kind in range(4):
                remote(kind, t).wait_send()

        @pl.when(me < NDEV)
        def _():
            for kind in range(4):
                form, ref, out = plan[kind]
                rows = BLK if kind in (0, 2) else WIN
                dst = out.at[pl.ds(pl.multiple_of(t * rows, rows), rows)]
                pltpu.make_async_remote_copy(
                    src_ref=dst,
                    dst_ref=dst,
                    send_sem=send_sem.at[kind, t],
                    recv_sem=recv_sem.at[kind, t],
                    device_id={"group": t},
                    device_id_type=MESH,
                ).wait_recv()

    @pl.when(me < NDEV)
    def _():
        for kind in range(4):
            local(kind).wait()


def attend_kernel(
    meta, kall, vall, qall, gall, tk_any, tv_any,
    gk_out, gv_out, gq_out, tk_out, tv_out,
    ks, vs, kt, qs, gs, s_buf, d_buf, p_buf, ds_buf, dq_acc, dq_buf, order, offs, sem,
):
    me = meta[NG]

    @pl.when(me < NDEV)
    def _():
        head = lax.div(me, 3)
        part = lax.rem(me, 3)
        cols = pl.ds(pl.multiple_of(head * DH, DH), DH)
        copy_k = pltpu.make_async_copy(tk_any.at[:, cols], ks.at[pl.ds(0, 2 * BLK)], sem.at[0])
        copy_v = pltpu.make_async_copy(tv_any.at[:, cols], vs.at[pl.ds(0, 2 * BLK)], sem.at[1])
        copy_k.start()
        copy_v.start()
        for s in range(NG):
            order[meta[s]] = s
        at = 0
        for r in range(NG):
            s = order[r]
            c = lax.rem(s, 3)
            offs[r] = at
            src = pl.multiple_of(s * WIN + jnp.where(part > c, 16, 0), 16)
            at = pl.multiple_of(at, 16) if r else 0
            qs[pl.ds(at, WIN), :] = qall[pl.ds(src, WIN), :]
            gs[pl.ds(at, WIN), :] = gall[pl.ds(src, WIN), :]
            at = at + jnp.where(part == c, 96, 80)
            rows = pl.ds(pl.multiple_of(s * BLK, BLK), BLK)
            ks[(r + 2) * BLK:(r + 3) * BLK, :] = kall[rows, :]
            vs[(r + 2) * BLK:(r + 3) * BLK, :] = vall[rows, :]
        at = pl.multiple_of(at, 16)
        qs[pl.ds(at, 48), :] = jnp.zeros((48, DH), BF16)
        gs[pl.ds(at, 48), :] = jnp.zeros((48, DH), BF16)
        copy_k.wait()
        copy_v.wait()

        @pl.loop(0, NG + 2)
        def _(ci):
            kt[ci] = ks[pl.ds(pl.multiple_of(ci * BLK, BLK), BLK), :].T

        def rank_at(row):
            rank = 0
            for r in range(1, NG):
                rank = rank + (row >= offs[r]).astype(jnp.int32)
            return rank

        def fold(x, op):
            return op(x.reshape(BLK // 8, 8, x.shape[-1]), axis=0)

        def rows_block(start, n):
            rows = pl.ds(start, n)
            qb = qs[rows, :]
            gb = gs[rows, :]
            low = rank_at(start)
            high = rank_at(start + n - 1)
            lanes = lax.broadcasted_iota(jnp.int32, (1, n), 1) + start
            row_rank = jnp.zeros((1, n), jnp.int32)
            for r in range(1, NG):
                row_rank = row_rank + (lanes >= offs[r]).astype(jnp.int32)

            def chunk(ci):
                return pl.ds(pl.multiple_of(ci * BLK, BLK), BLK)

            def scores(ci, top, masked):
                s = lax.dot_general(
                    ks[chunk(ci), :], qb, (((1,), (1,)), ((), ())), preferred_element_type=F32
                ) * (SCALE * math.log2(math.e))
                if masked:
                    s = jnp.where(row_rank >= ci - 2, s, -jnp.inf)
                s_buf[chunk(ci), 0:n] = s
                return jnp.maximum(top, fold(s, jnp.max))

            top = jnp.full((8, n), -jnp.inf, F32)
            top = lax.fori_loop(0, low + 3, lambda ci, t: scores(ci, t, False), top)
            top = lax.fori_loop(low + 3, high + 3, lambda ci, t: scores(ci, t, True), top)
            top = jnp.max(top, axis=0, keepdims=True)

            def weigh(ci, carry):
                e = jnp.exp2(s_buf[chunk(ci), 0:n] - top)
                dp = lax.dot_general(
                    vs[chunk(ci), :], gb, (((1,), (1,)), ((), ())), preferred_element_type=F32
                )
                s_buf[chunk(ci), 0:n] = e
                d_buf[chunk(ci), 0:n] = dp
                return carry[0] + fold(e, jnp.sum), carry[1] + fold(e * dp, jnp.sum)

            zero = jnp.zeros((8, n), F32)
            norm, inner = lax.fori_loop(0, high + 3, weigh, (zero, zero))
            inv = 1.0 / jnp.sum(norm, axis=0, keepdims=True)
            delta = jnp.sum(inner, axis=0, keepdims=True) * inv
            dq_acc[:, 0:n] = jnp.zeros((DH, n), F32)

            @pl.loop(0, high + 3)
            def _(ci):
                p = s_buf[chunk(ci), 0:n] * inv
                ds = (p * (d_buf[chunk(ci), 0:n] - delta) * SCALE).astype(BF16)
                p_buf[chunk(ci), rows] = p.astype(BF16)
                ds_buf[chunk(ci), rows] = ds
                dq_acc[:, 0:n] += jnp.dot(kt[ci], ds, preferred_element_type=F32)

            dq_buf[rows, :] = dq_acc[:, 0:n].T

        @pl.loop(0, 5)
        def _(b):
            rows_block(pl.multiple_of(b * BLK, BLK), BLK)

        rows_block(5 * BLK, 128)

        def grads(ci, first, put):
            keys = pl.ds(pl.multiple_of(ci * BLK, BLK), BLK)
            for b in range(6):
                @pl.when(first == b)
                def _():
                    rows = slice(b * BLK, ROWS)
                    put(
                        jnp.dot(ds_buf[keys, rows], qs[rows, :], preferred_element_type=F32),
                        jnp.dot(p_buf[keys, rows], gs[rows, :], preferred_element_type=F32),
                    )

        @pl.loop(0, 2)
        def _(ci):
            keys = pl.ds(pl.multiple_of(ci * BLK, BLK), BLK)
            rows = slice(0, ROWS)
            tk_out[keys, :] = jnp.dot(
                ds_buf[keys, rows], qs[rows, :], preferred_element_type=F32
            ).astype(BF16)
            tv_out[keys, :] = jnp.dot(
                p_buf[keys, rows], gs[rows, :], preferred_element_type=F32
            ).astype(BF16)

        @pl.loop(0, NG)
        def _(r):
            def put(gk, gv):
                place = pl.ds(pl.multiple_of(order[r] * BLK, BLK), BLK)
                gk_out[place, :] = gk.astype(BF16)
                gv_out[place, :] = gv.astype(BF16)

            grads(r + 2, lax.div(offs[r], BLK), put)
            src = pl.ds(pl.multiple_of(offs[r], 16), WIN)
            gq_out[pl.ds(pl.multiple_of(order[r] * WIN, WIN), WIN), :] = dq_buf[src, :].astype(BF16)


def text_start(part):
    return part * TWIN - 16 * (part // 2)


def return_kernel(
    nh, gk, gv, gq, tk, tv, q_ref, k_ref, gain_q, gain_k, scales,
    dq, dk, dv, dtk, dtv,
    got_k, got_v, got_q, text_in, text_sum, text_all, uq, uk, sq_send, sq_recv,
    send_sem, recv_sem, local_sem, trio_send, trio_recv, all_send, all_recv, ss, rs,
):
    me = lax.axis_index("group")
    hd = lax.axis_index("head")
    greet(me, hd, nh)
    part = lax.rem(me, 3)
    working = me < NDEV

    def trio(j, i):
        other = lax.rem(part + j, 3)
        start = pl.multiple_of(other * TWIN - 16 * lax.div(other, 2), 16)
        ref = (tk, tv)[i]
        return pltpu.make_async_remote_copy(
            src_ref=ref.at[pl.ds(start, TWIN)],
            dst_ref=text_in.at[j, i],
            send_sem=trio_send.at[j, i],
            recv_sem=trio_recv.at[j, i],
            device_id={"group": me - part + other},
            device_id_type=MESH,
        )

    def back(kind, t):
        ref, got = ((gk, got_k), (gv, got_v), (gq, got_q))[kind]
        n = (BLK, BLK, WIN)[kind]
        return ref.at[pl.ds(pl.multiple_of(t * n, n), n)], got.at[me]

    def back_remote(kind, t):
        src, dst = back(kind, t)
        return pltpu.make_async_remote_copy(
            src_ref=src,
            dst_ref=dst,
            send_sem=send_sem.at[kind, t],
            recv_sem=recv_sem.at[kind, me],
            device_id={"group": t},
            device_id_type=MESH,
        )

    def back_local(kind):
        src, dst = back(kind, me)
        return pltpu.make_async_copy(src, dst, local_sem.at[kind])

    def cast(t):
        return pltpu.make_async_remote_copy(
            src_ref=text_sum,
            dst_ref=text_all.at[me],
            send_sem=all_send.at[t],
            recv_sem=all_recv.at[me],
            device_id={"group": t},
            device_id_type=MESH,
        )

    @pl.when(working)
    def _():
        for j in (1, 2):
            for i in range(2):
                trio(j, i).start()

        @pl.loop(1, NG)
        def _(d):
            t = lax.rem(me + d, NG)
            for kind in range(3):
                back_remote(kind, t).start()

        for kind in range(3):
            back_local(kind).start()
        for j in (1, 2):
            for i in range(2):
                trio(j, i).wait()
        start = pl.multiple_of(part * TWIN - 16 * lax.div(part, 2), 16)
        for i in range(2):
            own = (tk, tv)[i][pl.ds(start, TWIN), :].astype(F32)
            text_sum[i] = (own + text_in[1, i].astype(F32) + text_in[2, i].astype(F32)).astype(BF16)

        @pl.loop(1, NG)
        def _(d):
            cast(lax.rem(me + d, NG)).start()

        text_all[me] = text_sum[...]
        for kind in range(3):
            back_local(kind).wait()

    @pl.loop(1, NG)
    def _(d):
        t = lax.rem(me + d, NG)

        @pl.when(t < NDEV)
        def _():
            for kind in range(3):
                got = (got_k, got_v, got_q)[kind]
                pltpu.make_async_remote_copy(
                    src_ref=got.at[t],
                    dst_ref=got.at[t],
                    send_sem=send_sem.at[kind, t],
                    recv_sem=recv_sem.at[kind, t],
                    device_id={"group": t},
                    device_id_type=MESH,
                ).wait_recv()

    acc_q = jnp.zeros((BLK, DH), F32)
    acc_k = jnp.zeros((BLK, DH), F32)
    c = lax.rem(me, 3)
    for h in range(NH):
        cols = slice(h * DH, (h + 1) * DH)
        for p in range(3):
            start = pl.multiple_of(p * 80 + jnp.where(p > c, 16, 0), 16)
            uq[pl.ds(start, WIN), cols] = got_q[3 * h + p].astype(F32) * gain_q[:, cols].astype(F32)
        u = got_k[3 * h].astype(F32) + got_k[3 * h + 1].astype(F32) + got_k[3 * h + 2].astype(F32)
        u = u * gain_k[:, cols].astype(F32)
        uk[:, cols] = u
        acc_k = acc_k + u * k_ref[:, cols].astype(F32)
        acc_q = acc_q + uq[0:BLK, cols] * q_ref[:, cols].astype(F32)
    copies = head_sum(row_sums(acc_q), row_sums(acc_k), sq_send, sq_recv, ss, rs, hd, nh)
    for h in range(NH):
        cols = slice(h * DH, (h + 1) * DH)
        dv[:, cols] = (
            got_v[3 * h].astype(F32) + got_v[3 * h + 1].astype(F32) + got_v[3 * h + 2].astype(F32)
        ).astype(BF16)
    inner = head_total(copies, sq_send, sq_recv, nh) / (NH * DH * nh)
    scale = scales[...]
    cube = scale * scale * scale * inner
    for row, u_ref, x_ref, out in ((0, uq, q_ref, dq), (1, uk, k_ref, dk)):
        col = as_column(scale[row:row + 1])
        col3 = as_column(cube[row:row + 1])
        for h in range(NH):
            cols = slice(h * DH, (h + 1) * DH)
            out[:, cols] = (col * u_ref[0:BLK, cols] - x_ref[:, cols].astype(F32) * col3).astype(BF16)

    @pl.loop(1, NG)
    def _(d):
        t = lax.rem(me + d, NG)

        @pl.when(t < NDEV)
        def _():
            pltpu.make_async_remote_copy(
                src_ref=text_all.at[t],
                dst_ref=text_all.at[t],
                send_sem=all_send.at[t],
                recv_sem=all_recv.at[t],
                device_id={"group": t},
                device_id_type=MESH,
            ).wait_recv()

    for i in range(NDEV):
        cols = slice((i // 3) * DH, (i // 3 + 1) * DH)
        rows = slice(text_start(i % 3), text_start(i % 3) + TWIN)
        dtk[rows, cols] = text_all[i, 0]
        dtv[rows, cols] = text_all[i, 1]

    @pl.when(working)
    def _():
        @pl.loop(1, NG)
        def _(d):
            t = lax.rem(me + d, NG)
            for kind in range(3):
                back_remote(kind, t).wait_send()
            cast(t).wait_send()


VM = pl.BlockSpec(memory_space=pltpu.VMEM)
SM = pl.BlockSpec(memory_space=pltpu.SMEM)
ANY = pl.BlockSpec(memory_space=pl.ANY)
DMA = pltpu.SemaphoreType.DMA


def shape(dims, dtype=BF16):
    return jax.ShapeDtypeStruct(dims, dtype)


def body(nh, queries, keys, values, text_keys, text_values, d_out, gain_q, gain_k, group_of):
    gain_q = gain_q[None, :]
    gain_k = gain_k[None, :]
    kall, vall, qall, gall, scales = pl.pallas_call(
        functools.partial(spread_kernel, nh),
        out_shape=(
            shape((NG * BLK, DH)), shape((NG * BLK, DH)), shape((QPAD, DH)), shape((QPAD, DH)),
            shape((8, BLK), F32),
        ),
        in_specs=[VM] * 6,
        out_specs=(ANY, ANY, ANY, ANY, VM),
        scratch_shapes=[
            pltpu.VMEM((BLK, NH * DH), BF16),
            pltpu.VMEM((BLK, NH * DH), BF16),
            pltpu.VMEM((8, BLK), F32),
            pltpu.VMEM((nh, 8, BLK), F32),
            DMA((4, NG)), DMA((4, NG)), DMA((4,)), DMA((nh,)), DMA((nh,)),
        ],
        compiler_params=pltpu.CompilerParams(
            collective_id=0, has_side_effects=True, vmem_limit_bytes=VMEM_LIMIT
        ),
        name="spread",
    )(queries, keys, values, d_out, gain_q, gain_k)

    meta = jnp.concatenate([group_of, lax.axis_index("group")[None].astype(jnp.int32)])
    gk, gv, gq, tk, tv = pl.pallas_call(
        attend_kernel,
        out_shape=(
            shape((NG * BLK, DH)), shape((NG * BLK, DH)), shape((NG * WIN, DH)),
            shape((2 * BLK, DH)), shape((2 * BLK, DH)),
        ),
        in_specs=[SM, VM, VM, VM, VM, ANY, ANY],
        out_specs=(VM,) * 5,
        scratch_shapes=[
            pltpu.VMEM(((NG + 2) * BLK, DH), BF16),
            pltpu.VMEM(((NG + 2) * BLK, DH), BF16),
            pltpu.VMEM((NG + 2, DH, BLK), BF16),
            pltpu.VMEM((ROWS + 32, DH), BF16),
            pltpu.VMEM((ROWS + 32, DH), BF16),
            pltpu.VMEM(((NG + 2) * BLK, BLK), F32),
            pltpu.VMEM(((NG + 2) * BLK, BLK), F32),
            pltpu.VMEM(((NG + 2) * BLK, ROWS), BF16),
            pltpu.VMEM(((NG + 2) * BLK, ROWS), BF16),
            pltpu.VMEM((DH, BLK), F32),
            pltpu.VMEM((ROWS + 32, DH), F32),
            pltpu.SMEM((NG,), jnp.int32),
            pltpu.SMEM((NG,), jnp.int32),
            DMA((2,)),
        ],
        compiler_params=pltpu.CompilerParams(vmem_limit_bytes=VMEM_LIMIT),
        name="attend",
    )(meta, kall, vall, qall, gall, text_keys, text_values)

    return pl.pallas_call(
        functools.partial(return_kernel, nh),
        out_shape=(
            shape((BLK, NH * DH)), shape((BLK, NH * DH)), shape((BLK, NH * DH)),
            shape((2 * BLK, NH * DH)), shape((2 * BLK, NH * DH)),
        ),
        in_specs=[ANY, ANY, ANY] + [VM] * 7,
        out_specs=(VM,) * 5,
        scratch_shapes=[
            pltpu.VMEM((NDEV, BLK, DH), BF16),
            pltpu.VMEM((NDEV, BLK, DH), BF16),
            pltpu.VMEM((NDEV, WIN, DH), BF16),
            pltpu.VMEM((3, 2, TWIN, DH), BF16),
            pltpu.VMEM((2, TWIN, DH), BF16),
            pltpu.VMEM((NG, 2, TWIN, DH), BF16),
            pltpu.VMEM((BLK + 16, NH * DH), F32),
            pltpu.VMEM((BLK, NH * DH), F32),
            pltpu.VMEM((8, BLK), F32),
            pltpu.VMEM((nh, 8, BLK), F32),
            DMA((3, NG)), DMA((3, NG)), DMA((3,)), DMA((3, 2)), DMA((3, 2)), DMA((NG,)), DMA((NG,)),
            DMA((nh,)), DMA((nh,)),
        ],
        compiler_params=pltpu.CompilerParams(
            collective_id=1, has_side_effects=True, vmem_limit_bytes=VMEM_LIMIT
        ),
        name="give_back",
    )(gk, gv, gq, tk, tv, queries, keys, gain_q, gain_k, scales)


def solution(mesh):
    placed = (
        P("group", "head"),
        P("group", "head"),
        P("group", "head"),
        P(None, "head"),
        P(None, "head"),
        P("group", "head"),
        P("head"),
        P("head"),
        P(),
    )
    return jax.shard_map(
        functools.partial(body, mesh.shape["head"]),
        mesh=mesh,
        in_specs=placed,
        out_specs=(
            P("group", "head"),
            P("group", "head"),
            P("group", "head"),
            P(None, "head"),
            P(None, "head"),
        ),
        check_vma=False,
    )
```

time: 554 us -> 182 us (0.33)
  the two profiles are of different devices: /device:TPU:4 before, /device:TPU:77 now
where the time goes in v1:
time: 182 us; the launch traced here: 181 us
  Pallas kernels  173 us (95%)
  local copies, waits for them, and re-layouts  7.31 us (4%)
    pallas_call x1, Pallas kernels, body(): pl.pallas_call(functools.partial(return_kernel, nh), out_shape=(shape((BL...  65.3 us
    pallas_call x1, Pallas kernels, body(): pl.pallas_call(attend_kernel, out_shape=(shape((NG * BLK, DH)), shape((NG...  58.5 us
    pallas_call x1, Pallas kernels, body(): pl.pallas_call(functools.partial(spread_kernel, nh), out_shape=(shape((NG...  48.8 us
    unnamed x19, local copies, waits for them, and re-layouts  6.15 us

profile of v1, /device:TPU:77, one launch (start us, length us, event | category | flops | bytes accessed | tf_op | source)
XLA Modules:
  0.0 181.2 jit_solution(2498726134098177968)
XLA Ops:
  0.6 0.0 copy-start.6
  0.6 0.0 copy-start.4
  0.7 0.6 copy-done.6
  1.3 0.7 pad_add_fusion.meta
  1.9 0.0 copy-done.4
  1.9 0.0 copy-start.5
  1.9 0.6 broadcast_in_dim.10.gain_q
  2.5 0.1 copy-done.5
  2.6 0.6 broadcast_in_dim.11.gain_k
  3.2 48.8 %spread.1 = (bf16[4096,128]{1,0:T(8,128)(2,1)}, bf16[4096,128]{1,0:T(8,128)(2,1)}, bf16[1552,128]{1,0:T(8,128)(2,1)}, bf16[1552,128]{1,0:T(8,128)(2,1)}, f32[8,256]{1,0:T(8,128)}) custom-call(bf16[256,640]{1,0:T(8,128)(2,1)} %q_ref.3, bf16[256,640]{1,0:T(8,128)(2,1)} %k_ref.3, bf16[256,640]{1,0:T(8,128)(2,1)} %v_ref.1, bf16[256,640]{1,0:T(8,128)(2,1)} %g_ref.1, ...), custom_call_target="tpu_custom_call" | custom-call | tf_op jit(solution)/shard_map/spread/pallas_call | solution.py:504
  52.0 58.5 %attend.1 = (bf16[4096,128]{1,0:T(8,128)(2,1)}, bf16[4096,128]{1,0:T(8,128)(2,1)}, bf16[1536,128]{1,0:T(8,128)(2,1)}, bf16[512,128]{1,0:T(8,128)(2,1)}, bf16[512,128]{1,0:T(8,128)(2,1)}) custom-call(s32[17]{0:T(128)} %pad_add_fusion.meta, bf16[4096,128]{1,0:T(8,128)(2,1)} %get-tuple-element.15.kall, bf16[4096,128]{1,0:T(8,128)(2,1)} %get-tuple-element.16.vall, ...), custom_call_target="tpu_custom_call" | custom-call | tf_op jit(solution)/shard_map/attend/pallas_call | solution.py:526
  110.5 65.3 %give_back.1 = (bf16[256,640]{1,0:T(8,128)(2,1)}, bf16[256,640]{1,0:T(8,128)(2,1)}, bf16[256,640]{1,0:T(8,128)(2,1)}, bf16[512,640]{1,0:T(8,128)(2,1)}, bf16[512,640]{1,0:T(8,128)(2,1)}) custom-call(bf16[4096,128]{1,0:T(8,128)(2,1)} %get-tuple-element.19.gk, bf16[4096,128]{1,0:T(8,128)(2,1)} %get-tuple-element.20.gv, ...), custom_call_target="tpu_custom_call" | custom-call | tf_op jit(solution)/shard_map/give_back/pallas_call | solution.py:554
  175.8 0.0 copy-start.3
  175.8 0.0 copy-start.2
  175.8 1.8 copy.19
  177.6 0.0 copy-done.3
  177.6 0.0 copy-start.1
  177.6 0.7 copy.20
  178.3 0.0 copy-done.2
  178.3 0.7 copy.21
  179.0 0.0 copy-done.1
  179.0 0.0 copy-start
  179.0 0.8 copy.22
  179.9 0.5 copy-done
  180.4 0.8 copy.23
Async XLA Ops:
  0.6 0.7 copy-start.6
  0.6 1.3 copy-start.4
  1.9 0.7 copy-start.5
  175.8 1.8 copy-start.3
  175.8 2.5 %copy-start.2 = (bf16[256,640]{1,0:T(8,128)(2,1)S(1)}, bf16[256,640]{1,0:T(8,128)(2,1)}, u32[]{:S(2)}) copy-start(bf16[256,640]{1,0:T(8,128)(2,1)} %get-tuple-element.32) | copy-start | bytes 983044
  177.6 1.5 copy-start.1
  179.0 1.3 copy-start

commit v2 on v0

v2 whole, which is shorter than its diff:
```python
import functools
import math

import jax
import jax.numpy as jnp
from jax import lax
from jax.experimental import pallas as pl
from jax.experimental.pallas import tpu as pltpu
from jax.sharding import PartitionSpec as P

DH = 128
EPS = 1e-06
BLK = 256
NG = 16
NH = 5
NDEV = 15
KC = 512
NP = 9
ROWS = 1536
SCALE = DH ** (-0.5)
LOG = SCALE * math.log2(math.e)
MESH = pl.DeviceIdType.MESH
F32 = jnp.float32
BF16 = jnp.bfloat16
VMEM_LIMIT = 62 * 1024 * 1024


def greet(me, hd, nh):
    barrier = pltpu.get_barrier_semaphore()
    for d in range(1, NG):
        pl.semaphore_signal(
            barrier, inc=1, device_id={"group": lax.rem(me + d, NG)}, device_id_type=MESH
        )
    for d in range(1, nh):
        pl.semaphore_signal(
            barrier, inc=1, device_id={"head": lax.rem(hd + d, nh)}, device_id_type=MESH
        )
    pl.semaphore_wait(barrier, NG - 1 + nh - 1)


def row_sums(acc):
    return jnp.sum(acc.T, axis=0, keepdims=True)


def as_column(row):
    return jnp.broadcast_to(row, (DH, BLK)).T


def head_sum(row_q, row_k, send, recv, send_sem, recv_sem, hd, nh):
    send[...] = jnp.concatenate([row_q, row_k, jnp.zeros((6, BLK), F32)], axis=0)
    copies = []
    for d in range(1, nh):
        peer = lax.rem(hd + d, nh)
        copy = pltpu.make_async_remote_copy(
            src_ref=send,
            dst_ref=recv.at[d],
            send_sem=send_sem.at[d],
            recv_sem=recv_sem.at[d],
            device_id={"head": peer},
            device_id_type=MESH,
        )
        copy.start()
        copies.append(copy)
    return copies


def head_total(copies, send, recv, nh):
    for copy in copies:
        copy.wait()
    total = send[...]
    for d in range(1, nh):
        total = total + recv[d]
    return total


def roles(t):
    h = lax.div(t, 3)
    odd = lax.rem(h, 2)
    return h, t - 3 * h, 3 * h + odd, 3 * h + 2 - 2 * odd


def push(src, dst, send_sem, recv_sem, t):
    return pltpu.make_async_remote_copy(
        src_ref=src, dst_ref=dst, send_sem=send_sem, recv_sem=recv_sem,
        device_id={"group": t}, device_id_type=MESH,
    )


def await_recv(dst, send_sem, recv_sem, t):
    push(dst, dst, send_sem, recv_sem, t).wait_recv()


def head_cols(h):
    return pl.ds(pl.multiple_of(h * DH, DH), DH)


def block(i, n):
    return pl.ds(pl.multiple_of(i * n, n), n)


def by_third(part, run):
    pl.when(part == 0)(lambda: run(96))
    pl.when(part > 0)(lambda: run(80))


def attend_kernel(
    nh, q_ref, k_ref, v_ref, g_ref, tk_ref, tv_ref, gain_q_ref, gain_k_ref, group_of, order,
    dq, dk, dv, dtk, dtv,
    qn, kn, kall, vall, qall, gall, ks, vs, kt, qs, gs, s_buf, d_buf, p_buf, ds_buf, dq_buf, dq_rank,
    tk, tv, pair_in, pair_sum, got, got_q, text_in, text_sum, text_all, uq, uk, sq_send, sq_recv,
    in_send, in_recv, relay_sem, local_sem, text_sem,
    pair_send, pair_recv, out_send, out_recv, q_send, q_recv, q_local,
    text_send, text_recv, cast_send, cast_recv, relay_send, mate_send, ss, rs,
):
    me = lax.axis_index("group")
    hd = lax.axis_index("head")
    core = lax.rem(me, 2)
    mate = me + 1 - 2 * core
    mirror = me + 2 - 4 * lax.rem(lax.div(me, 2), 2)
    my_head, my_part, my_pair, my_single = roles(me)
    working = me < NDEV
    alone = working & (me == my_single)
    paired = working & (me != my_single)
    size = jnp.where(my_part == 0, 96, 80)
    blocks = jnp.where(my_part == 0, 6, 5)
    gain_q = gain_q_ref[...].astype(F32)[None, :]
    gain_k = gain_k_ref[...].astype(F32)[None, :]

    def text_copy(i):
        return pltpu.make_async_copy(
            (tk_ref, tv_ref)[i].at[:, head_cols(my_head)], (ks, vs)[i].at[pl.ds(0, KC)],
            text_sem.at[i])

    pl.when(working)(lambda: [text_copy(i).start() for i in range(2)] and None)
    greet(me, hd, nh)

    whole = ((0, v_ref, vall), (2, kn, kall))
    thirds = ((1, g_ref, gall), (3, qn, qall))

    def third_src(ref, h, part, size):
        start = 0 if size == 96 else pl.multiple_of(part * 80 + 16, 16)
        return ref.at[pl.ds(start, size), head_cols(h)]

    def to_all(stage, act):
        kind, ref, out = whole[stage]
        kind3, ref3, out3 = thirds[stage]

        @pl.loop(1, NG)
        def _(d):
            t = lax.rem(me + d, NG)

            @pl.when(t < NDEV)
            def _():
                h, part, pair, single = roles(t)

                @pl.when((t == single) | (t == pair + core))
                def _():
                    act(push(ref.at[:, head_cols(h)], out.at[me],
                             in_send.at[kind, t], in_recv.at[kind, me], t))

                by_third(part, lambda size: act(
                    push(third_src(ref3, h, part, size), out3.at[me, pl.ds(0, size)],
                         in_send.at[kind3, t], in_recv.at[kind3, me], t)))

    def to_self(stage, act):
        kind, ref, out = whole[stage]
        kind3, ref3, out3 = thirds[stage]

        @pl.when(working)
        def _():
            act(pltpu.make_async_copy(
                ref.at[:, head_cols(my_head)], out.at[me], local_sem.at[kind]))
            by_third(my_part, lambda size: act(pltpu.make_async_copy(
                third_src(ref3, my_head, my_part, size), out3.at[me, pl.ds(0, size)],
                local_sem.at[kind3])))

    def start(copy):
        copy.start()

    def relay(stage, s):
        kind, ref, out = whole[stage]
        view = out.at[s]
        return push(view, view, relay_sem.at[kind, s], in_recv.at[kind, s], mate)

    def relay_all(stage):
        kind, ref, out = whole[stage]

        @pl.when(paired)
        def _():
            relay(stage, me).start()

            @pl.loop(1, 8)
            def _(d):
                s = lax.rem(me + NG - 2 * d, NG)
                await_recv(out.at[s], in_send.at[kind, s], in_recv.at[kind, s], s)
                relay(stage, s).start()

    acc_q = jnp.zeros((BLK, DH), F32)
    acc_k = jnp.zeros((BLK, DH), F32)
    for h in range(NH):
        cols = slice(h * DH, (h + 1) * DH)
        x = q_ref[:, cols].astype(F32)
        acc_q = acc_q + x * x
        x = k_ref[:, cols].astype(F32)
        acc_k = acc_k + x * x
    copies = head_sum(row_sums(acc_q), row_sums(acc_k), sq_send.at[0], sq_recv.at[0], ss.at[0], rs.at[0], hd, nh)
    to_all(0, start)
    to_self(0, start)
    total = head_total(copies, sq_send.at[0], sq_recv.at[0], nh)
    scale = lax.rsqrt(total / (NH * DH * nh) + EPS)
    col_q = as_column(scale[0:1])
    col_k = as_column(scale[1:2])
    for h in range(NH):
        cols = slice(h * DH, (h + 1) * DH)
        kn[:, cols] = (k_ref[:, cols].astype(F32) * col_k * gain_k[:, cols]).astype(BF16)
        qn[:, cols] = (q_ref[:, cols].astype(F32) * col_q * gain_q[:, cols]).astype(BF16)
    to_all(1, start)
    to_self(1, start)

    @pl.loop(0, blocks)
    def _(b):
        @pl.loop(lax.div(lax.div(b * BLK + BLK - 1, size), 2) + 2, NP)
        def _(i):
            for j in range(2):
                p_buf[b, 2 * i + j] = jnp.zeros((BLK, BLK), BF16)
                ds_buf[b, 2 * i + j] = jnp.zeros((BLK, BLK), BF16)

    to_self(0, lambda copy: copy.wait())
    relay_all(0)
    to_self(1, lambda copy: copy.wait())
    relay_all(1)

    @pl.when(working)
    def _():
        @pl.loop(1, NG)
        def _(d):
            s = lax.rem(me + d, NG)
            for kind, ref, out in whole:
                @pl.when((me == my_single) | (lax.rem(d, 2) == 1))
                def _():
                    await_recv(
                        out.at[s], in_send.at[kind, s], in_recv.at[kind, s], s)
            for kind, ref, out in thirds:
                by_third(my_part, lambda size: await_recv(
                    out.at[s, pl.ds(0, size)], in_send.at[kind, s], in_recv.at[kind, s], s))

    @pl.when(paired)
    def _():
        @pl.loop(0, 8)
        def _(d):
            s = lax.rem(me + 2 * d, NG)
            for stage in range(2):
                relay(stage, s).wait_send()

    for stage in range(2):
        to_all(stage, lambda copy: copy.wait_send())

    @pl.when(working)
    def _():
        for i in range(2):
            text_copy(i).wait()

        def gather(n):
            for r in range(NG):
                qs[r * n:(r + 1) * n, :] = qall[order[r], 0:n, :]
                gs[r * n:(r + 1) * n, :] = gall[order[r], 0:n, :]

        by_third(my_part, gather)
        for r in range(NG):
            ks[(r + 2) * BLK:(r + 3) * BLK, :] = kall[order[r]]
            vs[(r + 2) * BLK:(r + 3) * BLK, :] = vall[order[r]]
        for i in range(NP):
            kt[i] = ks[i * KC:(i + 1) * KC, :].T

        def fold(x, op):
            return op(x.reshape(x.shape[0] // 8, 8, x.shape[-1]), axis=0)

        def rows_block(blk, start, n):
            rows = pl.ds(start, BLK)
            q_cols = qs[rows, :].T
            g_cols = gs[rows, :].T
            lanes = lax.broadcasted_iota(jnp.int32, (1, BLK), 1) + start
            row_rank = jnp.zeros((1, BLK), jnp.int32)
            for r in range(1, NG):
                row_rank = row_rank + (lanes >= r * size).astype(jnp.int32)
            at = [slice(i * KC, (i + 1) * KC) for i in range(n)]
            top = jnp.full((1, BLK), -jnp.inf, F32)
            norm = jnp.zeros((8, BLK), F32)
            inner = jnp.zeros((8, BLK), F32)
            tops = []
            for i in range(n):
                s = jnp.dot(ks[at[i], :], q_cols, preferred_element_type=F32)
                dp = jnp.dot(vs[at[i], :], g_cols, preferred_element_type=F32)
                if i > max(0, (n - 1) - 3):
                    s = jnp.concatenate(
                        [
                            jnp.where(row_rank >= 2 * i - 2, s[0:BLK], -jnp.inf),
                            jnp.where(row_rank >= 2 * i - 1, s[BLK:KC], -jnp.inf),
                        ],
                        axis=0,
                    )
                new = jnp.maximum(top, jnp.max(fold(s, jnp.max), axis=0, keepdims=True) * LOG)
                e = jnp.exp2(s * LOG - new)
                s_buf[at[i], :] = e
                d_buf[at[i], :] = dp
                shrink = jnp.exp2(top - new)
                norm = norm * shrink + fold(e, jnp.sum)
                inner = inner * shrink + fold(e * dp, jnp.sum)
                top = new
                tops.append(new)
            inv = 1.0 / jnp.sum(norm, axis=0, keepdims=True)
            delta = jnp.sum(inner, axis=0, keepdims=True) * inv
            dq = jnp.zeros((DH, BLK), F32)
            for i in range(n):
                p = s_buf[at[i], :] * (jnp.exp2(tops[i] - top) * inv)
                ds = (p * (d_buf[at[i], :] - delta)).astype(BF16)
                soft = p.astype(BF16)
                for j in range(2):
                    p_buf[blk, 2 * i + j] = soft[j * BLK:(j + 1) * BLK]
                    ds_buf[blk, 2 * i + j] = ds[j * BLK:(j + 1) * BLK]
                dq = dq + jnp.dot(kt[i], ds, preferred_element_type=F32)
            dq_buf[rows, :] = dq.T * SCALE

        @pl.loop(0, blocks)
        def _(b):
            start = pl.multiple_of(b * BLK, BLK)
            pairs = lax.div(lax.div(start + BLK - 1, size), 2) + 2
            for n in range(3, NP + 1):
                pl.when(pairs == n)(functools.partial(rows_block, b, start, n))

    parts = (kall, vall)
    texts = (tk, tv)

    def wait_send(copy):
        copy.wait_send()

    def to_mate(i, j):
        s = 2 * j + 1 - core
        return push(parts[i].at[s], pair_in.at[i, j],
                    pair_send.at[i, j], pair_recv.at[i, j], mate)

    def text_to(i, t, slot):
        return push(texts[i], text_in.at[slot], text_send.at[i], text_recv.at[slot], t)

    def gq_out(t, size):
        return push(qall.at[t, pl.ds(0, size)], got_q.at[me, pl.ds(0, size)],
                    q_send.at[t], q_recv.at[me], t)

    def gq_self(size):
        return pltpu.make_async_copy(
            qall.at[me, pl.ds(0, size)], got_q.at[me, pl.ds(0, size)], q_local)

    def single_out(i, t):
        return push(parts[i].at[t], got.at[i, 2 * my_head + 1],
                    out_send.at[i, t], out_recv.at[i, 2 * my_head + 1], t)

    def pair_out(i, j):
        return push(pair_sum.at[i, j], got.at[i, 2 * my_head],
                    out_send.at[i, 2 * j + core], out_recv.at[i, 2 * my_head], 2 * j + core)

    def cast(t, n):
        return push(text_sum, text_all.at[my_head, core],
                    cast_send.at[n], cast_recv.at[my_head, core], t)

    def pass_on(h, t, sem):
        view = text_all.at[h, core]
        return push(view, view, sem, cast_recv.at[h, core], t)

    def await_text(h, kind):
        view = text_all.at[h, kind]
        await_recv(view, cast_send.at[0], cast_recv.at[h, kind], mate)

    def pair_text(act):
        pl.when(core == 0)(lambda: act(text_to(1, mate, 0)))
        pl.when(core == 1)(lambda: act(text_to(0, mate, 0)))

    def single_text(act):
        act(text_to(0, my_pair, 1))
        act(text_to(1, my_pair + 1, 1))

    def grads(chunk, last):
        gk = gv = 0
        for b in range(last):
            rows = slice(b * BLK, (b + 1) * BLK)
            gk = gk + jnp.dot(ds_buf[b, chunk], qs[rows, :], preferred_element_type=F32)
            gv = gv + jnp.dot(p_buf[b, chunk], gs[rows, :], preferred_element_type=F32)
        return gk * SCALE, gv

    def give(n):
        last = 6 if n == 96 else 5
        for r in range(NG):
            dq_rank[r, 0:n] = dq_buf[r * n:(r + 1) * n, :].astype(BF16)
        for s in range(NG):
            qall[s, 0:n] = dq_rank[group_of[s], 0:n]

        @pl.loop(1, NG)
        def _(d):
            gq_out(lax.rem(me + d, NG), n).start()

        gq_self(n).start()
        for i in range(2):
            gk, gv = grads(i, last)
            tk[i * BLK:(i + 1) * BLK, :] = gk.astype(BF16)
            tv[i * BLK:(i + 1) * BLK, :] = gv.astype(BF16)

        @pl.when(paired)
        def _():
            pair_text(start)

        pl.when(alone)(lambda: single_text(start))

        def half(parity, put):
            @pl.loop(0, 8)
            def _(n):
                j = lax.rem(lax.div(me, 2) + n, 8)
                t = 2 * j + parity
                put(j, t, grads(group_of[t] + 2, last))

        def keep(j, t, pair):
            for i in range(2):
                parts[i][t] = pair[i].astype(BF16)
            pl.when(paired)(lambda: [to_mate(i, j).start() for i in range(2)] and None)
            pl.when(alone & (t != me))(lambda: [single_out(i, t).start() for i in range(2)] and None)

            @pl.when(alone & (t == me))
            def _():
                for i in range(2):
                    got[i, 2 * my_head + 1] = pair[i].astype(BF16)

        def join(j, t, pair):
            for i in range(2):
                await_recv(pair_in.at[i, j], pair_send.at[i, j], pair_recv.at[i, j], mate)
                pair_sum[i, j] = (pair[i] + pair_in[i, j].astype(F32)).astype(BF16)

            @pl.when(t != me)
            def _():
                for i in range(2):
                    pair_out(i, j).start()

            @pl.when(t == me)
            def _():
                for i in range(2):
                    got[i, 2 * my_head] = pair_sum[i, j]

        half(1 - core, keep)

        @pl.when(paired)
        def _():
            for slot in range(2):
                await_recv(text_in.at[slot], text_send.at[0], text_recv.at[slot], mate)
            other = text_in[0].astype(F32) + text_in[1].astype(F32)

            @pl.when(core == 0)
            def _():
                text_sum[...] = (tk[...].astype(F32) + other).astype(BF16)

            @pl.when(core == 1)
            def _():
                text_sum[...] = (tv[...].astype(F32) + other).astype(BF16)

            cast(mirror, 0).start()
            for n in (1, 2, 3):
                cast(lax.rem(me + 4 * n, NG), n).start()
            text_all[my_head, core] = text_sum[...]
            half(core, join)

        pl.when(alone)(lambda: half(core, keep))

    pl.when(working)(lambda: by_third(my_part, give))

    for h in range(NH):
        source = 3 * h + h % 2 + core

        @pl.when(mirror == source)
        def _():
            await_text(h, core)
            for n in (1, 2, 3):
                pass_on(h, lax.rem(me + 4 * n, NG), relay_send.at[n]).start()

    for h in range(NH):
        source = 3 * h + h % 2 + core
        pl.when((mirror != source) & (me != source))(lambda: await_text(h, core))
        pass_on(h, mate, mate_send.at[h]).start()

    pl.when(working)(lambda: by_third(my_part, lambda size: gq_self(size).wait()))
    acc_q = jnp.zeros((BLK, DH), F32)
    acc_k = jnp.zeros((BLK, DH), F32)
    for h in range(NH):
        cols = slice(h * DH, (h + 1) * DH)
        pair = 3 * h + h % 2 + core
        single = 3 * h + 2 - 2 * (h % 2)
        for i in range(2):
            for slot, src in ((2 * h, pair), (2 * h + 1, single)):
                pl.when(src != me)(lambda: await_recv(
                    got.at[i, slot], out_send.at[i, 0], out_recv.at[i, slot], src))
        for p, at, size in ((0, 0, 96), (1, 96, 80), (2, 176, 80)):
            src = 3 * h + p
            pl.when(src != me)(lambda: await_recv(
                got_q.at[src, pl.ds(0, size)], q_send.at[0], q_recv.at[src], src))
            uq[at:at + size, cols] = got_q[src, 0:size].astype(F32) * gain_q[:, cols]
        u = (got[0, 2 * h].astype(F32) + got[0, 2 * h + 1].astype(F32)) * gain_k[:, cols]
        uk[:, cols] = u
        acc_k = acc_k + u * k_ref[:, cols].astype(F32)
        acc_q = acc_q + uq[:, cols] * q_ref[:, cols].astype(F32)
    copies = head_sum(row_sums(acc_q), row_sums(acc_k), sq_send.at[1], sq_recv.at[1], ss.at[1], rs.at[1], hd, nh)
    for h in range(NH):
        cols = slice(h * DH, (h + 1) * DH)
        dv[:, cols] = (got[1, 2 * h].astype(F32) + got[1, 2 * h + 1].astype(F32)).astype(BF16)
    for h in range(NH):
        cols = slice(h * DH, (h + 1) * DH)
        await_text(h, 1 - core)
        dtk[:, cols] = text_all[h, 0]
        dtv[:, cols] = text_all[h, 1]
    inner = head_total(copies, sq_send.at[1], sq_recv.at[1], nh) / (NH * DH * nh)
    cube = scale * scale * scale * inner
    for row, u_ref, x_ref, out in ((0, uq, q_ref, dq), (1, uk, k_ref, dk)):
        col = as_column(scale[row:row + 1])
        col3 = as_column(cube[row:row + 1])
        for h in range(NH):
            cols = slice(h * DH, (h + 1) * DH)
            out[:, cols] = (col * u_ref[:, cols] - x_ref[:, cols].astype(F32) * col3).astype(BF16)

    for h in range(NH):
        source = 3 * h + h % 2 + core
        pass_on(h, mate, mate_send.at[h]).wait_send()

        @pl.when(mirror == source)
        def _():
            for n in (1, 2, 3):
                pass_on(h, lax.rem(me + 4 * n, NG), relay_send.at[n]).wait_send()

    pl.when(alone)(lambda: single_text(wait_send))

    @pl.when(paired)
    def _():
        pair_text(wait_send)
        for n in range(4):
            cast(mate, n).wait_send()

        @pl.loop(0, 8)
        def _(j):
            for i in range(2):
                to_mate(i, j).wait_send()
                pl.when(2 * j + core != me)(lambda: pair_out(i, j).wait_send())

    @pl.when(working)
    def _():
        @pl.loop(1, NG)
        def _(d):
            t = lax.rem(me + d, NG)

            @pl.when(alone)
            def _():
                for i in range(2):
                    single_out(i, t).wait_send()

            by_third(my_part, lambda size: gq_out(t, size).wait_send())


def final_kernel(*refs):
    n = len(refs) // 2
    for src, dst in zip(refs[:n], refs[n:]):
        dst[...] = src[...]


VM = pl.BlockSpec(memory_space=pltpu.VMEM)
SM = pl.BlockSpec(memory_space=pltpu.SMEM)
ANY = pl.BlockSpec(memory_space=pl.ANY)
DMA = pltpu.SemaphoreType.DMA


def body(nh, queries, keys, values, text_keys, text_values, d_out, gain_q, gain_k, group_of):
    results = tuple(
        jax.ShapeDtypeStruct((n, NH * DH), BF16) for n in (BLK, BLK, BLK, 2 * BLK, 2 * BLK)
    )
    places = jnp.arange(NG, dtype=jnp.int32)
    order = jnp.sum(jnp.where(group_of[None, :] == places[:, None], places[None, :], 0), axis=1)
    grads = pl.pallas_call(
        functools.partial(attend_kernel, nh),
        out_shape=results,
        in_specs=[VM] * 4 + [ANY] * 2 + [VM] * 2 + [SM] * 2,
        out_specs=(VM,) * 5,
        scratch_shapes=[
            pltpu.VMEM((BLK, NH * DH), BF16),
            pltpu.VMEM((BLK, NH * DH), BF16),
            pltpu.VMEM((NG, BLK, DH), BF16),
            pltpu.VMEM((NG, BLK, DH), BF16),
            pltpu.VMEM((NG, 96, DH), BF16),
            pltpu.VMEM((NG, 96, DH), BF16),
            pltpu.VMEM((NP * KC, DH), BF16),
            pltpu.VMEM((NP * KC, DH), BF16),
            pltpu.VMEM((NP, DH, KC), BF16),
            pltpu.VMEM((ROWS, DH), BF16),
            pltpu.VMEM((ROWS, DH), BF16),
            pltpu.VMEM((NP * KC, BLK), F32),
            pltpu.VMEM((NP * KC, BLK), F32),
            pltpu.VMEM((6, 2 * NP, BLK, BLK), BF16),
            pltpu.VMEM((6, 2 * NP, BLK, BLK), BF16),
            pltpu.VMEM((ROWS, DH), F32),
            pltpu.VMEM((NG, 96, DH), BF16),
            pltpu.VMEM((KC, DH), BF16),
            pltpu.VMEM((KC, DH), BF16),
            pltpu.VMEM((2, 8, BLK, DH), BF16),
            pltpu.VMEM((2, 8, BLK, DH), BF16),
            pltpu.VMEM((2, 2 * NH, BLK, DH), BF16),
            pltpu.VMEM((NDEV, 96, DH), BF16),
            pltpu.VMEM((2, 2 * BLK, DH), BF16),
            pltpu.VMEM((2 * BLK, DH), BF16),
            pltpu.VMEM((NH, 2, 2 * BLK, DH), BF16),
            pltpu.VMEM((BLK, NH * DH), F32),
            pltpu.VMEM((BLK, NH * DH), F32),
            pltpu.VMEM((2, 8, BLK), F32),
            pltpu.VMEM((2, nh, 8, BLK), F32),
            DMA((4, NG)), DMA((4, NG)), DMA((4, NG)), DMA((4,)), DMA((2,)),
            DMA((2, 8)), DMA((2, 8)), DMA((2, NG)), DMA((2, 2 * NH)), DMA((NG,)), DMA((NG,)),
            DMA, DMA((2,)), DMA((2,)), DMA((4,)), DMA((NH, 2)), DMA((4,)), DMA((NH,)),
            DMA((2, nh)), DMA((2, nh)),
        ],
        compiler_params=pltpu.CompilerParams(
            collective_id=0, has_side_effects=True, vmem_limit_bytes=VMEM_LIMIT
        ),
        name="attend",
    )(queries, keys, values, d_out, text_keys, text_values, gain_q, gain_k, group_of, order)
    return pl.pallas_call(
        final_kernel,
        out_shape=results,
        in_specs=[VM] * 5,
        out_specs=(VM,) * 5,
        name="finish",
    )(*grads)


def solution(mesh):
    placed = (
        P("group", "head"),
        P("group", "head"),
        P("group", "head"),
        P(None, "head"),
        P(None, "head"),
        P("group", "head"),
        P("head"),
        P("head"),
        P(),
    )
    return jax.shard_map(
        functools.partial(body, mesh.shape["head"]),
        mesh=mesh,
        in_specs=placed,
        out_specs=(
            P("group", "head"),
            P("group", "head"),
            P("group", "head"),
            P(None, "head"),
            P(None, "head"),
        ),
        check_vma=False,
    )
```

time: 554 us -> 109 us (0.20)
  the two profiles are of different devices: /device:TPU:4 before, /device:TPU:1 now
where the time goes in v2:
time: 109 us
  Pallas kernels  107 us (98%)
  other arithmetic  1.28 us (1%)
    pallas_call x1, Pallas kernels, body(): pl.pallas_call(functools.partial(attend_kernel, nh), out_shape=results, i...  104 us
    pallas_call x1, Pallas kernels, body(): pl.pallas_call(final_kernel, out_shape=results, in_specs=[VM] * 5, out_sp...  3.04 us

profile of v2, /device:TPU:1, one launch (start us, length us, event | category | flops | bytes accessed | tf_op | source)
XLA Modules:
  0.0 109.0 jit_solution(8826396571974831966)
XLA Ops:
  0.6 1.3 %select_reduce_fusion.order = s32[16]{0:T(128)} fusion(s32[16]{0:T(128)} %group_of.1), kind=kLoop, calls=%fused_computation | loop fusion | flops 752 | bytes 128 | tf_op jit(solution)/shard_map/reduce_sum | solution.py:577
  1.9 104.1 %attend.1 = (bf16[256,640]{1,0:T(8,128)(2,1)}, bf16[256,640]{1,0:T(8,128)(2,1)}, bf16[256,640]{1,0:T(8,128)(2,1)}, bf16[512,640]{1,0:T(8,128)(2,1)}, bf16[512,640]{1,0:T(8,128)(2,1)}) custom-call(bf16[256,640]{1,0:T(8,128)(2,1)} %q_ref.1, bf16[256,640]{1,0:T(8,128)(2,1)} %k_ref.1, bf16[256,640]{1,0:T(8,128)(2,1)} %v_ref.1, bf16[256,640]{1,0:T(8,128)(2,1)} %g_ref.1, ...), custom_call_target="tpu_custom_call" | custom-call | tf_op jit(solution)/shard_map/attend/pallas_call | solution.py:578
  106.0 3.0 %finish.1 = (bf16[256,640]{1,0:T(8,128)(2,1)}, bf16[256,640]{1,0:T(8,128)(2,1)}, bf16[256,640]{1,0:T(8,128)(2,1)}, bf16[512,640]{1,0:T(8,128)(2,1)}, bf16[512,640]{1,0:T(8,128)(2,1)}) custom-call(bf16[256,640]{1,0:T(8,128)(2,1)} %get-tuple-element.10.refs_0_, bf16[256,640]{1,0:T(8,128)(2,1)} %get-tuple-element.11.refs_1_, ...), custom_call_target="tpu_custom_call" | custom-call | tf_op jit(solution)/shard_map/finish/pallas_call | solution.py:624

commit v3 on v2

v3 whole, which is shorter than its diff:
```python
import functools
import math

import jax
import jax.numpy as jnp
from jax import lax
from jax.experimental import pallas as pl
from jax.experimental.pallas import tpu as pltpu
from jax.sharding import PartitionSpec as P

DH = 128
EPS = 1e-06
BLK = 256
NG = 16
NH = 5
HALF = 128
NB = 8
KC = 512
NP = 9
ROWS = 2048
SCALE = DH ** (-0.5)
LOG = SCALE * math.log2(math.e)
MESH = pl.DeviceIdType.MESH
F32 = jnp.float32
BF16 = jnp.bfloat16
VMEM_LIMIT = 62 * 1024 * 1024


def greet(me, hd, nh):
    barrier = pltpu.get_barrier_semaphore()
    for d in range(1, NG):
        pl.semaphore_signal(
            barrier, inc=1, device_id={"group": lax.rem(me + d, NG)}, device_id_type=MESH
        )
    for d in range(1, nh):
        pl.semaphore_signal(
            barrier, inc=1, device_id={"head": lax.rem(hd + d, nh)}, device_id_type=MESH
        )
    pl.semaphore_wait(barrier, NG - 1 + nh - 1)


def row_sums(acc):
    return jnp.sum(acc.T, axis=0, keepdims=True)


def as_column(row):
    return jnp.broadcast_to(row, (DH, BLK)).T


def head_sum(row_q, row_k, send, recv, send_sem, recv_sem, hd, nh):
    send[...] = jnp.concatenate([row_q, row_k, jnp.zeros((6, BLK), F32)], axis=0)
    copies = []
    for d in range(1, nh):
        peer = lax.rem(hd + d, nh)
        copy = pltpu.make_async_remote_copy(
            src_ref=send,
            dst_ref=recv.at[d],
            send_sem=send_sem.at[d],
            recv_sem=recv_sem.at[d],
            device_id={"head": peer},
            device_id_type=MESH,
        )
        copy.start()
        copies.append(copy)
    return copies


def head_total(copies, send, recv, nh):
    for copy in copies:
        copy.wait()
    total = send[...]
    for d in range(1, nh):
        total = total + recv[d]
    return total


def base_of(h):
    return 2 * (h + 2 * (h // 3))


def push(src, dst, send_sem, recv_sem, t):
    return pltpu.make_async_remote_copy(
        src_ref=src, dst_ref=dst, send_sem=send_sem, recv_sem=recv_sem,
        device_id={"group": t}, device_id_type=MESH,
    )


def await_recv(dst, send_sem, recv_sem, t):
    push(dst, dst, send_sem, recv_sem, t).wait_recv()


def head_cols(h):
    return pl.ds(pl.multiple_of(h * DH, DH), DH)


def attend_kernel(
    nh, q_ref, k_ref, v_ref, g_ref, tk_ref, tv_ref, gain_q_ref, gain_k_ref, group_of, order,
    dq, dk, dv, dtk, dtv,
    qn, kn, kall, vall, qall, gall, ks, vs, kt, qs, gs, s_buf, d_buf, p_bufs, ds_bufs, dq_buf, dq_rank,
    tk, tv, pair_in, pair_sum, got, got_q, text_in, text_sum, text_all, uq, uk, sq_send, sq_recv,
    in_send, in_recv, relay_sem, local_sem, text_sem,
    pair_send, pair_recv, out_send, out_recv, q_send, q_recv, q_local,
    text_send, text_recv, cast_send, cast_recv, relay_send, mate_send, ss, rs,
):
    me = lax.axis_index("group")
    hd = lax.axis_index("head")
    core = lax.rem(me, 2)
    mate = me + 1 - 2 * core
    mirror = me + 2 - 4 * lax.rem(lax.div(me, 2), 2)
    chip = lax.div(me, 2)
    my_head = chip - 2 * lax.div(chip, 5)
    working = (chip < 3) | (chip == 5) | (chip == 6)
    gain_q = gain_q_ref[...].astype(F32)[None, :]
    gain_k = gain_k_ref[...].astype(F32)[None, :]

    def text_copy(i):
        return pltpu.make_async_copy(
            (tk_ref, tv_ref)[i].at[:, head_cols(my_head)], (ks, vs)[i].at[pl.ds(0, KC)],
            text_sem.at[i])

    pl.when(working)(lambda: [text_copy(i).start() for i in range(2)] and None)
    greet(me, hd, nh)

    whole = ((0, v_ref, vall), (2, kn, kall))
    halves = ((1, g_ref, gall), (3, qn, qall))

    def half_src(ref, h, part):
        return ref.at[pl.ds(pl.multiple_of(part * HALF, HALF), HALF), head_cols(h)]

    def to_all(stage, act):
        kind, ref, out = whole[stage]
        kind2, ref2, out2 = halves[stage]

        @pl.loop(0, NH)
        def _(d):
            h = lax.rem(my_head + 1 + d, NH)
            base = 2 * (h + 2 * lax.div(h, 3))

            @pl.when(base + core != me)
            def _():
                act(push(ref.at[:, head_cols(h)], out.at[me],
                         in_send.at[kind, 2 * h + core], in_recv.at[kind, me], base + core))

            for part in range(2):
                @pl.when(base + part != me)
                def _():
                    act(push(half_src(ref2, h, part), out2.at[me],
                             in_send.at[kind2, 2 * h + part], in_recv.at[kind2, me], base + part))

    def to_self(stage, act):
        kind, ref, out = whole[stage]
        kind2, ref2, out2 = halves[stage]

        @pl.when(working)
        def _():
            act(pltpu.make_async_copy(
                ref.at[:, head_cols(my_head)], out.at[me], local_sem.at[kind]))
            act(pltpu.make_async_copy(
                half_src(ref2, my_head, core), out2.at[me], local_sem.at[kind2]))

    def start(copy):
        copy.start()

    def relay(stage, s):
        kind, ref, out = whole[stage]
        view = out.at[s]
        return push(view, view, relay_sem.at[kind, s], in_recv.at[kind, s], mate)

    def relay_all(stage):
        kind, ref, out = whole[stage]

        @pl.when(working)
        def _():
            relay(stage, me).start()

            @pl.loop(1, 8)
            def _(d):
                s = lax.rem(me + NG - 2 * d, NG)
                await_recv(out.at[s], in_send.at[kind, 0], in_recv.at[kind, s], s)
                relay(stage, s).start()

    acc_q = jnp.zeros((BLK, DH), F32)
    acc_k = jnp.zeros((BLK, DH), F32)
    for h in range(NH):
        cols = slice(h * DH, (h + 1) * DH)
        x = q_ref[:, cols].astype(F32)
        acc_q = acc_q + x * x
        x = k_ref[:, cols].astype(F32)
        acc_k = acc_k + x * x
    copies = head_sum(row_sums(acc_q), row_sums(acc_k), sq_send.at[0], sq_recv.at[0], ss.at[0], rs.at[0], hd, nh)
    to_all(0, start)
    to_self(0, start)
    total = head_total(copies, sq_send.at[0], sq_recv.at[0], nh)
    scale = lax.rsqrt(total / (NH * DH * nh) + EPS)
    col_q = as_column(scale[0:1])
    col_k = as_column(scale[1:2])
    for h in range(NH):
        cols = slice(h * DH, (h + 1) * DH)
        kn[:, cols] = (k_ref[:, cols].astype(F32) * col_k * gain_k[:, cols]).astype(BF16)
        qn[:, cols] = (q_ref[:, cols].astype(F32) * col_q * gain_q[:, cols]).astype(BF16)
    to_all(1, start)
    to_self(1, start)

    to_self(0, lambda copy: copy.wait())
    relay_all(0)
    to_self(1, lambda copy: copy.wait())
    relay_all(1)

    @pl.when(working)
    def _():
        @pl.loop(1, NG)
        def _(d):
            s = lax.rem(me + d, NG)

            @pl.when(lax.rem(d, 2) == 1)
            def _():
                for kind, ref, out in whole:
                    await_recv(out.at[s], in_send.at[kind, 0], in_recv.at[kind, s], s)

            for kind, ref, out in halves:
                await_recv(out.at[s], in_send.at[kind, 0], in_recv.at[kind, s], s)

    @pl.when(working)
    def _():
        @pl.loop(0, 8)
        def _(d):
            s = lax.rem(me + 2 * d, NG)
            for stage in range(2):
                relay(stage, s).wait_send()

    for stage in range(2):
        to_all(stage, lambda copy: copy.wait_send())

    @pl.when(working)
    def _():
        for i in range(2):
            text_copy(i).wait()

        for r in range(NG):
            qs[r * HALF:(r + 1) * HALF, :] = qall[order[r]]
            gs[r * HALF:(r + 1) * HALF, :] = gall[order[r]]
        for r in range(NG):
            ks[(r + 2) * BLK:(r + 3) * BLK, :] = kall[order[r]]
            vs[(r + 2) * BLK:(r + 3) * BLK, :] = vall[order[r]]
        for i in range(NP):
            kt[i] = ks[i * KC:(i + 1) * KC, :].T

        def fold(x, op):
            return op(x.reshape(x.shape[0] // 8, 8, x.shape[-1]), axis=0)

        def rows_block(b):
            n = b + 2
            rows = slice(b * BLK, (b + 1) * BLK)
            q_cols = qs[rows, :].T
            g_cols = gs[rows, :].T
            later = lax.broadcasted_iota(jnp.int32, (1, BLK), 1) >= HALF
            at = [slice(i * KC, (i + 1) * KC) for i in range(n)]
            top = jnp.full((1, BLK), -jnp.inf, F32)
            norm = jnp.zeros((8, BLK), F32)
            inner = jnp.zeros((8, BLK), F32)
            tops = []
            for i in range(n):
                s = jnp.dot(ks[at[i], :], q_cols, preferred_element_type=F32)
                dp = jnp.dot(vs[at[i], :], g_cols, preferred_element_type=F32)
                if i == n - 1:
                    s = jnp.concatenate([s[0:BLK], jnp.where(later, s[BLK:KC], -jnp.inf)], axis=0)
                new = jnp.maximum(top, jnp.max(fold(s, jnp.max), axis=0, keepdims=True) * LOG)
                e = jnp.exp2(s * LOG - new)
                s_buf[at[i], :] = e
                d_buf[at[i], :] = dp
                shrink = jnp.exp2(top - new)
                norm = norm * shrink + fold(e, jnp.sum)
                inner = inner * shrink + fold(e * dp, jnp.sum)
                top = new
                tops.append(new)
            inv = 1.0 / jnp.sum(norm, axis=0, keepdims=True)
            delta = jnp.sum(inner, axis=0, keepdims=True) * inv
            dq = jnp.zeros((DH, BLK), F32)
            for i in range(n):
                p = s_buf[at[i], :] * (jnp.exp2(tops[i] - top) * inv)
                ds = (p * (d_buf[at[i], :] - delta)).astype(BF16)
                soft = p.astype(BF16)
                for j in range(2):
                    p_bufs[b][2 * i + j] = soft[j * BLK:(j + 1) * BLK]
                    ds_bufs[b][2 * i + j] = ds[j * BLK:(j + 1) * BLK]
                dq = dq + jnp.dot(kt[i], ds, preferred_element_type=F32)
            dq_buf[rows, :] = dq.T * SCALE

        for b in range(NB):
            rows_block(b)

    parts = (kall, vall)
    texts = (tk, tv)

    def wait_send(copy):
        copy.wait_send()

    def to_mate(i, j):
        return push(parts[i].at[2 * j + 1 - core], pair_in.at[i, j],
                    pair_send.at[i, j], pair_recv.at[i, j], mate)

    def text_to(i):
        return push(texts[i], text_in, text_send, text_recv, mate)

    def gq_out(t):
        return push(qall.at[t], got_q.at[2 * my_head + core],
                    q_send.at[t], q_recv.at[2 * my_head + core], t)

    def gq_self():
        return pltpu.make_async_copy(qall.at[me], got_q.at[2 * my_head + core], q_local)

    def pair_out(i, j):
        return push(pair_sum.at[i, j], got.at[i, my_head],
                    out_send.at[i, j], out_recv.at[i, my_head], 2 * j + core)

    def cast(t, n):
        return push(text_sum, text_all.at[my_head, core],
                    cast_send.at[n], cast_recv.at[my_head, core], t)

    def pass_on(h, t, sem):
        view = text_all.at[h, core]
        return push(view, view, sem, cast_recv.at[h, core], t)

    def await_text(h, kind):
        view = text_all.at[h, kind]
        await_recv(view, cast_send.at[0], cast_recv.at[h, kind], mate)

    def pair_text(act):
        pl.when(core == 0)(lambda: act(text_to(1)))
        pl.when(core == 1)(lambda: act(text_to(0)))

    def grads(chunk):
        gk = gv = 0
        for b in range(NB):
            rows = slice(b * BLK, (b + 1) * BLK)
            last = 2 * b + 3
            index = jnp.minimum(chunk, last)
            here_k = jnp.dot(ds_bufs[b][index], qs[rows, :], preferred_element_type=F32)
            here_v = jnp.dot(p_bufs[b][index], gs[rows, :], preferred_element_type=F32)
            if b < NB - 1:
                seen = (chunk <= last).astype(F32)
                here_k, here_v = here_k * seen, here_v * seen
            gk, gv = gk + here_k, gv + here_v
        return gk * SCALE, gv

    @pl.when(working)
    def _():
        for r in range(NG):
            dq_rank[r] = dq_buf[r * HALF:(r + 1) * HALF, :].astype(BF16)
        for s in range(NG):
            qall[s] = dq_rank[group_of[s]]

        @pl.loop(1, NG)
        def _(d):
            gq_out(lax.rem(me + d, NG)).start()

        gq_self().start()

        @pl.loop(0, 2)
        def _(i):
            gk, gv = grads(i)
            place = pl.ds(pl.multiple_of(i * BLK, BLK), BLK)
            tk[place, :] = gk.astype(BF16)
            tv[place, :] = gv.astype(BF16)

        pair_text(start)

        def each(put):
            @pl.loop(0, 8)
            def _(n):
                put(lax.rem(chip + n, 8))

        def keep(j):
            t = 2 * j + 1 - core
            pair = grads(group_of[t] + 2)
            for i in range(2):
                parts[i][t] = pair[i].astype(BF16)
                to_mate(i, j).start()

        def join(j):
            t = 2 * j + core
            pair = grads(group_of[t] + 2)
            for i in range(2):
                await_recv(pair_in.at[i, j], pair_send.at[i, j], pair_recv.at[i, j], mate)
                pair_sum[i, j] = (pair[i] + pair_in[i, j].astype(F32)).astype(BF16)
                pl.when(t != me)(lambda: pair_out(i, j).start())

                @pl.when(t == me)
                def _():
                    got[i, my_head] = pair_sum[i, j]

        each(keep)
        await_recv(text_in, text_send, text_recv, mate)

        @pl.when(core == 0)
        def _():
            text_sum[...] = (tk[...].astype(F32) + text_in[...].astype(F32)).astype(BF16)

        @pl.when(core == 1)
        def _():
            text_sum[...] = (tv[...].astype(F32) + text_in[...].astype(F32)).astype(BF16)

        cast(mirror, 0).start()
        for n in (1, 2, 3):
            cast(lax.rem(me + 4 * n, NG), n).start()
        text_all[my_head, core] = text_sum[...]
        each(join)

    for h in range(NH):
        source = base_of(h) + core

        @pl.when(mirror == source)
        def _():
            await_text(h, core)
            for n in (1, 2, 3):
                pass_on(h, lax.rem(me + 4 * n, NG), relay_send.at[n]).start()

    for h in range(NH):
        source = base_of(h) + core
        pl.when((mirror != source) & (me != source))(lambda: await_text(h, core))
        pass_on(h, mate, mate_send.at[h]).start()

    pl.when(working)(lambda: gq_self().wait())
    acc_q = jnp.zeros((BLK, DH), F32)
    acc_k = jnp.zeros((BLK, DH), F32)
    for h in range(NH):
        cols = slice(h * DH, (h + 1) * DH)
        for i in range(2):
            pl.when(base_of(h) + core != me)(lambda: await_recv(
                got.at[i, h], out_send.at[i, 0], out_recv.at[i, h], base_of(h) + core))
        for p in range(2):
            pl.when(base_of(h) + p != me)(lambda: await_recv(
                got_q.at[2 * h + p], q_send.at[0], q_recv.at[2 * h + p], base_of(h) + p))
            uq[p * HALF:(p + 1) * HALF, cols] = got_q[2 * h + p].astype(F32) * gain_q[:, cols]
        u = got[0, h].astype(F32) * gain_k[:, cols]
        uk[:, cols] = u
        acc_k = acc_k + u * k_ref[:, cols].astype(F32)
        acc_q = acc_q + uq[:, cols] * q_ref[:, cols].astype(F32)
    copies = head_sum(row_sums(acc_q), row_sums(acc_k), sq_send.at[1], sq_recv.at[1], ss.at[1], rs.at[1], hd, nh)
    for h in range(NH):
        cols = slice(h * DH, (h + 1) * DH)
        dv[:, cols] = got[1, h]
    for h in range(NH):
        cols = slice(h * DH, (h + 1) * DH)
        await_text(h, 1 - core)
        dtk[:, cols] = text_all[h, 0]
        dtv[:, cols] = text_all[h, 1]
    inner = head_total(copies, sq_send.at[1], sq_recv.at[1], nh) / (NH * DH * nh)
    cube = scale * scale * scale * inner
    for row, u_ref, x_ref, out in ((0, uq, q_ref, dq), (1, uk, k_ref, dk)):
        col = as_column(scale[row:row + 1])
        col3 = as_column(cube[row:row + 1])
        for h in range(NH):
            cols = slice(h * DH, (h + 1) * DH)
            out[:, cols] = (col * u_ref[:, cols] - x_ref[:, cols].astype(F32) * col3).astype(BF16)

    for h in range(NH):
        source = base_of(h) + core
        pass_on(h, mate, mate_send.at[h]).wait_send()

        @pl.when(mirror == source)
        def _():
            for n in (1, 2, 3):
                pass_on(h, lax.rem(me + 4 * n, NG), relay_send.at[n]).wait_send()

    @pl.when(working)
    def _():
        pair_text(wait_send)
        for n in range(4):
            cast(mate, n).wait_send()

        @pl.loop(0, 8)
        def _(j):
            for i in range(2):
                to_mate(i, j).wait_send()
                pl.when(2 * j + core != me)(lambda: pair_out(i, j).wait_send())

        @pl.loop(1, NG)
        def _(d):
            gq_out(lax.rem(me + d, NG)).wait_send()


def final_kernel(*refs):
    n = len(refs) // 2
    for src, dst in zip(refs[:n], refs[n:]):
        dst[...] = src[...]


VM = pl.BlockSpec(memory_space=pltpu.VMEM)
SM = pl.BlockSpec(memory_space=pltpu.SMEM)
ANY = pl.BlockSpec(memory_space=pl.ANY)
DMA = pltpu.SemaphoreType.DMA


def body(nh, queries, keys, values, text_keys, text_values, d_out, gain_q, gain_k, group_of):
    results = tuple(
        jax.ShapeDtypeStruct((n, NH * DH), BF16) for n in (BLK, BLK, BLK, 2 * BLK, 2 * BLK)
    )
    places = jnp.arange(NG, dtype=jnp.int32)
    order = jnp.sum(jnp.where(group_of[None, :] == places[:, None], places[None, :], 0), axis=1)
    grads = pl.pallas_call(
        functools.partial(attend_kernel, nh),
        out_shape=results,
        in_specs=[VM] * 4 + [ANY] * 2 + [VM] * 2 + [SM] * 2,
        out_specs=(VM,) * 5,
        scratch_shapes=[
            pltpu.VMEM((BLK, NH * DH), BF16),
            pltpu.VMEM((BLK, NH * DH), BF16),
            pltpu.VMEM((NG, BLK, DH), BF16),
            pltpu.VMEM((NG, BLK, DH), BF16),
            pltpu.VMEM((NG, HALF, DH), BF16),
            pltpu.VMEM((NG, HALF, DH), BF16),
            pltpu.VMEM((NP * KC, DH), BF16),
            pltpu.VMEM((NP * KC, DH), BF16),
            pltpu.VMEM((NP, DH, KC), BF16),
            pltpu.VMEM((ROWS, DH), BF16),
            pltpu.VMEM((ROWS, DH), BF16),
            pltpu.VMEM((NP * KC, BLK), F32),
            pltpu.VMEM((NP * KC, BLK), F32),
            [pltpu.VMEM((2 * b + 4, BLK, BLK), BF16) for b in range(NB)],
            [pltpu.VMEM((2 * b + 4, BLK, BLK), BF16) for b in range(NB)],
            pltpu.VMEM((ROWS, DH), F32),
            pltpu.VMEM((NG, HALF, DH), BF16),
            pltpu.VMEM((KC, DH), BF16),
            pltpu.VMEM((KC, DH), BF16),
            pltpu.VMEM((2, 8, BLK, DH), BF16),
            pltpu.VMEM((2, 8, BLK, DH), BF16),
            pltpu.VMEM((2, NH, BLK, DH), BF16),
            pltpu.VMEM((2 * NH, HALF, DH), BF16),
            pltpu.VMEM((2 * BLK, DH), BF16),
            pltpu.VMEM((2 * BLK, DH), BF16),
            pltpu.VMEM((NH, 2, 2 * BLK, DH), BF16),
            pltpu.VMEM((BLK, NH * DH), F32),
            pltpu.VMEM((BLK, NH * DH), F32),
            pltpu.VMEM((2, 8, BLK), F32),
            pltpu.VMEM((2, nh, 8, BLK), F32),
            DMA((4, NG)), DMA((4, NG)), DMA((4, NG)), DMA((4,)), DMA((2,)),
            DMA((2, 8)), DMA((2, 8)), DMA((2, 8)), DMA((2, NH)), DMA((NG,)), DMA((2 * NH,)),
            DMA, DMA, DMA, DMA((4,)), DMA((NH, 2)), DMA((4,)), DMA((NH,)),
            DMA((2, nh)), DMA((2, nh)),
        ],
        compiler_params=pltpu.CompilerParams(
            collective_id=0, has_side_effects=True, vmem_limit_bytes=VMEM_LIMIT
        ),
        name="attend",
    )(queries, keys, values, d_out, text_keys, text_values, gain_q, gain_k, group_of, order)
    return pl.pallas_call(
        final_kernel,
        out_shape=results,
        in_specs=[VM] * 5,
        out_specs=(VM,) * 5,
        name="finish",
    )(*grads)


def solution(mesh):
    placed = (
        P("group", "head"),
        P("group", "head"),
        P("group", "head"),
        P(None, "head"),
        P(None, "head"),
        P("group", "head"),
        P("head"),
        P("head"),
        P(),
    )
    return jax.shard_map(
        functools.partial(body, mesh.shape["head"]),
        mesh=mesh,
        in_specs=placed,
        out_specs=(
            P("group", "head"),
            P("group", "head"),
            P("group", "head"),
            P(None, "head"),
            P(None, "head"),
        ),
        check_vma=False,
    )
```

time: 109 us -> 99.2 us (0.910)
  the two profiles are of different devices: /device:TPU:1 before, /device:TPU:4 now
where the time goes in v3:
time: 99.2 us; the launch traced here: 99.1 us
  Pallas kernels  97.1 us (98%)
  other arithmetic  1.28 us (1%)
    pallas_call x1, Pallas kernels, body(): pl.pallas_call(functools.partial(attend_kernel, nh), out_shape=results, i...  94.1 us
    pallas_call x1, Pallas kernels, body(): pl.pallas_call(final_kernel, out_shape=results, in_specs=[VM] * 5, out_sp...  3.04 us

profile of v3, /device:TPU:4, one launch (start us, length us, event | category | flops | bytes accessed | tf_op | source)
XLA Modules:
  0.0 99.1 jit_solution(2462542593046321440)
XLA Ops:
  0.6 1.3 %select_reduce_fusion.order = s32[16]{0:T(128)} fusion(s32[16]{0:T(128)} %group_of.1), kind=kLoop, calls=%fused_computation | loop fusion | flops 752 | bytes 128 | tf_op jit(solution)/shard_map/reduce_sum | solution.py:500
  1.9 94.1 %attend.1 = (bf16[256,640]{1,0:T(8,128)(2,1)}, bf16[256,640]{1,0:T(8,128)(2,1)}, bf16[256,640]{1,0:T(8,128)(2,1)}, bf16[512,640]{1,0:T(8,128)(2,1)}, bf16[512,640]{1,0:T(8,128)(2,1)}) custom-call(bf16[256,640]{1,0:T(8,128)(2,1)} %q_ref.1, bf16[256,640]{1,0:T(8,128)(2,1)} %k_ref.1, bf16[256,640]{1,0:T(8,128)(2,1)} %v_ref.1, bf16[256,640]{1,0:T(8,128)(2,1)} %g_ref.1, ...), custom_call_target="tpu_custom_call" | custom-call | tf_op jit(solution)/shard_map/attend/pallas_call | solution.py:501
  96.0 3.0 %finish.1 = (bf16[256,640]{1,0:T(8,128)(2,1)}, bf16[256,640]{1,0:T(8,128)(2,1)}, bf16[256,640]{1,0:T(8,128)(2,1)}, bf16[512,640]{1,0:T(8,128)(2,1)}, bf16[512,640]{1,0:T(8,128)(2,1)}) custom-call(bf16[256,640]{1,0:T(8,128)(2,1)} %get-tuple-element.10.refs_0_, bf16[256,640]{1,0:T(8,128)(2,1)} %get-tuple-element.11.refs_1_, ...), custom_call_target="tpu_custom_call" | custom-call | tf_op jit(solution)/shard_map/finish/pallas_call | solution.py:547

commit v4 on v3

--- a/solution.py
+++ b/solution.py
@@ -36,7 +36,7 @@
         pl.semaphore_signal(
             barrier, inc=1, device_id={"head": lax.rem(hd + d, nh)}, device_id_type=MESH
         )
-    pl.semaphore_wait(barrier, NG - 1 + nh - 1)
+    return lambda: pl.semaphore_wait(barrier, NG - 1 + nh - 1)
 
 
 def row_sums(acc):
@@ -94,7 +94,7 @@
 
 
 def attend_kernel(
-    nh, q_ref, k_ref, v_ref, g_ref, tk_ref, tv_ref, gain_q_ref, gain_k_ref, group_of, order,
+    nh, q_ref, k_ref, v_ref, g_ref, tk_ref, tv_ref, gain_q_ref, gain_k_ref, group_of,
     dq, dk, dv, dtk, dtv,
     qn, kn, kall, vall, qall, gall, ks, vs, kt, qs, gs, s_buf, d_buf, p_bufs, ds_bufs, dq_buf, dq_rank,
     tk, tv, pair_in, pair_sum, got, got_q, text_in, text_sum, text_all, uq, uk, sq_send, sq_recv,
@@ -119,7 +119,7 @@
             text_sem.at[i])
 
     pl.when(working)(lambda: [text_copy(i).start() for i in range(2)] and None)
-    greet(me, hd, nh)
+    met = greet(me, hd, nh)
 
     whole = ((0, v_ref, vall), (2, kn, kall))
     halves = ((1, g_ref, gall), (3, qn, qall))
@@ -187,7 +187,14 @@
         acc_q = acc_q + x * x
         x = k_ref[:, cols].astype(F32)
         acc_k = acc_k + x * x
-    copies = head_sum(row_sums(acc_q), row_sums(acc_k), sq_send.at[0], sq_recv.at[0], ss.at[0], rs.at[0], hd, nh)
+    sums = row_sums(acc_q), row_sums(acc_k)
+    order = [
+        jnp.minimum(
+            sum((group_of[t] == r).astype(jnp.int32) * t for t in range(1, NG)), NG - 1)
+        for r in range(NG)
+    ]
+    met()
+    copies = head_sum(*sums, sq_send.at[0], sq_recv.at[0], ss.at[0], rs.at[0], hd, nh)
     to_all(0, start)
     to_self(0, start)
     total = head_total(copies, sq_send.at[0], sq_recv.at[0], nh)
@@ -365,11 +372,6 @@
 
         pair_text(start)
 
-        def each(put):
-            @pl.loop(0, 8)
-            def _(n):
-                put(lax.rem(chip + n, 8))
-
         def keep(j):
             t = 2 * j + 1 - core
             pair = grads(group_of[t] + 2)
@@ -389,7 +391,7 @@
                 def _():
                     got[i, my_head] = pair_sum[i, j]
 
-        each(keep)
+        keep(chip)
         await_recv(text_in, text_send, text_recv, mate)
 
         @pl.when(core == 0)
@@ -404,7 +406,13 @@
         for n in (1, 2, 3):
             cast(lax.rem(me + 4 * n, NG), n).start()
         text_all[my_head, core] = text_sum[...]
-        each(join)
+
+        @pl.loop(1, 8)
+        def _(n):
+            keep(lax.rem(chip + n, 8))
+            join(lax.rem(chip + n - 1, 8))
+
+        join(lax.rem(chip + 7, 8))
 
     for h in range(NH):
         source = base_of(h) + core
@@ -481,9 +489,22 @@
 
 
 def final_kernel(*refs):
-    n = len(refs) // 2
-    for src, dst in zip(refs[:n], refs[n:]):
-        dst[...] = src[...]
+    n = 5
+    held, sem = refs[2 * n:3 * n], refs[3 * n]
+    pieces = [(i, at) for i in range(n) for at in range(0, refs[i].shape[0], BLK)]
+
+    def copy(k, src, dst, way):
+        i, at = pieces[k]
+        rows = pl.ds(at, BLK)
+        return pltpu.make_async_copy(src[i].at[rows], dst[i].at[rows], sem.at[way, k])
+
+    for k in range(len(pieces)):
+        copy(k, refs[:n], held, 0).start()
+    for k in range(len(pieces)):
+        copy(k, refs[:n], held, 0).wait()
+        copy(k, held, refs[n:2 * n], 1).start()
+    for k in range(len(pieces)):
+        copy(k, held, refs[n:2 * n], 1).wait()
 
 
 VM = pl.BlockSpec(memory_space=pltpu.VMEM)
@@ -496,12 +517,10 @@
     results = tuple(
         jax.ShapeDtypeStruct((n, NH * DH), BF16) for n in (BLK, BLK, BLK, 2 * BLK, 2 * BLK)
     )
-    places = jnp.arange(NG, dtype=jnp.int32)
-    order = jnp.sum(jnp.where(group_of[None, :] == places[:, None], places[None, :], 0), axis=1)
     grads = pl.pallas_call(
         functools.partial(attend_kernel, nh),
         out_shape=results,
-        in_specs=[VM] * 4 + [ANY] * 2 + [VM] * 2 + [SM] * 2,
+        in_specs=[VM] * 4 + [ANY] * 2 + [VM] * 2 + [SM],
         out_specs=(VM,) * 5,
         scratch_shapes=[
             pltpu.VMEM((BLK, NH * DH), BF16),
@@ -543,12 +562,13 @@
             collective_id=0, has_side_effects=True, vmem_limit_bytes=VMEM_LIMIT
         ),
         name="attend",
-    )(queries, keys, values, d_out, text_keys, text_values, gain_q, gain_k, group_of, order)
+    )(queries, keys, values, d_out, text_keys, text_values, gain_q, gain_k, group_of)
     return pl.pallas_call(
         final_kernel,
         out_shape=results,
-        in_specs=[VM] * 5,
-        out_specs=(VM,) * 5,
+        in_specs=[ANY] * 5,
+        out_specs=(ANY,) * 5,
+        scratch_shapes=[pltpu.VMEM(r.shape, BF16) for r in results] + [DMA((2, 7))],
         name="finish",
     )(*grads)
 

time: 99.2 us -> 95.9 us (0.967)
  Pallas kernels: 97.1 us -> 94.9 us
  other arithmetic: 1.28 us -> 0 us
    pallas_call x1, Pallas kernels: 94.1 us -> 92.5 us  [body(): pl.pallas_call(functools.partial(attend_kernel, nh), out_shape=results, i...]
    reduce_sum x1 -> x0, other arithmetic: 1.28 us -> none  [body(): jnp.sum(jnp.where(group_of[None, :] == places[:, None], places[None, :],...]
where the time goes in v4:
time: 95.9 us; the launch traced here: 95.8 us
  Pallas kernels  94.9 us (99%)
    pallas_call x1, Pallas kernels, body(): pl.pallas_call(functools.partial(attend_kernel, nh), out_shape=results, i...  92.5 us
    pallas_call x1, Pallas kernels, body(): pl.pallas_call(final_kernel, out_shape=results, in_specs=[ANY] * 5, out_s...  2.47 us

profile of v4, /device:TPU:4, one launch (start us, length us, event | category | flops | bytes accessed | tf_op | source)
XLA Modules:
  0.0 95.8 jit_solution(7594072812514460296)
XLA Ops:
  0.6 92.5 %attend.1 = (bf16[256,640]{1,0:T(8,128)(2,1)}, bf16[256,640]{1,0:T(8,128)(2,1)}, bf16[256,640]{1,0:T(8,128)(2,1)}, bf16[512,640]{1,0:T(8,128)(2,1)}, bf16[512,640]{1,0:T(8,128)(2,1)}) custom-call(bf16[256,640]{1,0:T(8,128)(2,1)} %q_ref.1, bf16[256,640]{1,0:T(8,128)(2,1)} %k_ref.1, bf16[256,640]{1,0:T(8,128)(2,1)} %v_ref.1, bf16[256,640]{1,0:T(8,128)(2,1)} %g_ref.1, ...), custom_call_target="tpu_custom_call" | custom-call | tf_op jit(solution)/shard_map/attend/pallas_call | solution.py:520
  93.1 2.5 %finish.1 = (bf16[256,640]{1,0:T(8,128)(2,1)}, bf16[256,640]{1,0:T(8,128)(2,1)}, bf16[256,640]{1,0:T(8,128)(2,1)}, bf16[512,640]{1,0:T(8,128)(2,1)}, bf16[512,640]{1,0:T(8,128)(2,1)}) custom-call(bf16[256,640]{1,0:T(8,128)(2,1)} %get-tuple-element.10.refs_0_, bf16[256,640]{1,0:T(8,128)(2,1)} %get-tuple-element.11.refs_1_, ...), custom_call_target="tpu_custom_call" | custom-call | tf_op jit(solution)/shard_map/finish/pallas_call | solution.py:566

commit v5 on v4

--- a/solution.py
+++ b/solution.py
@@ -226,17 +226,6 @@
 
             for kind, ref, out in halves:
                 await_recv(out.at[s], in_send.at[kind, 0], in_recv.at[kind, s], s)
-
-    @pl.when(working)
-    def _():
-        @pl.loop(0, 8)
-        def _(d):
-            s = lax.rem(me + 2 * d, NG)
-            for stage in range(2):
-                relay(stage, s).wait_send()
-
-    for stage in range(2):
-        to_all(stage, lambda copy: copy.wait_send())
 
     @pl.when(working)
     def _():
@@ -295,6 +284,17 @@
 
         for b in range(NB):
             rows_block(b)
+
+    @pl.when(working)
+    def _():
+        @pl.loop(0, 8)
+        def _(d):
+            s = lax.rem(me + 2 * d, NG)
+            for stage in range(2):
+                relay(stage, s).wait_send()
+
+    for stage in range(2):
+        to_all(stage, lambda copy: copy.wait_send())
 
     parts = (kall, vall)
     texts = (tk, tv)

time: 95.9 us -> 94.4 us (0.984)
  Pallas kernels: 94.9 us -> 92.7 us
    pallas_call x1, Pallas kernels: 92.5 us -> 90.2 us  [body(): pl.pallas_call(functools.partial(attend_kernel, nh), out_shape=results, i...]
where the time goes in v5:
time: 94.4 us; the launch traced here: 93.5 us
  Pallas kernels  92.7 us (98%)
    pallas_call x1, Pallas kernels, body(): pl.pallas_call(functools.partial(attend_kernel, nh), out_shape=results, i...  90.2 us
    pallas_call x1, Pallas kernels, body(): pl.pallas_call(final_kernel, out_shape=results, in_specs=[ANY] * 5, out_s...  2.47 us

profile of v5, /device:TPU:4, one launch (start us, length us, event | category | flops | bytes accessed | tf_op | source)
XLA Modules:
  0.0 93.5 jit_solution(7510307457277408308)
XLA Ops:
  0.6 90.2 %attend.1 = (bf16[256,640]{1,0:T(8,128)(2,1)}, bf16[256,640]{1,0:T(8,128)(2,1)}, bf16[256,640]{1,0:T(8,128)(2,1)}, bf16[512,640]{1,0:T(8,128)(2,1)}, bf16[512,640]{1,0:T(8,128)(2,1)}) custom-call(bf16[256,640]{1,0:T(8,128)(2,1)} %q_ref.1, bf16[256,640]{1,0:T(8,128)(2,1)} %k_ref.1, bf16[256,640]{1,0:T(8,128)(2,1)} %v_ref.1, bf16[256,640]{1,0:T(8,128)(2,1)} %g_ref.1, ...), custom_call_target="tpu_custom_call" | custom-call | tf_op jit(solution)/shard_map/attend/pallas_call | solution.py:520
  90.8 2.5 %finish.1 = (bf16[256,640]{1,0:T(8,128)(2,1)}, bf16[256,640]{1,0:T(8,128)(2,1)}, bf16[256,640]{1,0:T(8,128)(2,1)}, bf16[512,640]{1,0:T(8,128)(2,1)}, bf16[512,640]{1,0:T(8,128)(2,1)}) custom-call(bf16[256,640]{1,0:T(8,128)(2,1)} %get-tuple-element.10.refs_0_, bf16[256,640]{1,0:T(8,128)(2,1)} %get-tuple-element.11.refs_1_, ...), custom_call_target="tpu_custom_call" | custom-call | tf_op jit(solution)/shard_map/finish/pallas_call | solution.py:566
